TPU v7x, 32 devices: a whole 2x2x4 slice. The times are simulated.
32 devices in a mesh: parts: 2 (over y), wide: 4 (over z), rep: 2 (over x), sub: 2 (over core).
Axes of the slice: x: 2, y: 2, z: 4, core: 2. Of those that a mesh axis runs over, the one named last changes fastest.
Arguments:
- activations: bfloat16 [8, 2048, 512], P(('parts', 'wide'), 'sub'), parts along dimension 0, may hold values from -6 to 6
- deltas: bfloat16 [8, 2048, 512], P(('parts', 'wide'), 'sub'), parts along dimension 0, may hold values from -6 to 6
- act_factor: bfloat16 [512, 512], P(None, 'rep'), as said below
- delta_factor: bfloat16 [512, 512], P(None, 'rep'), as said below
- queries: bfloat16 [1280, 512, 512], P(None, ('rep', 'wide'), 'sub'), may hold values from -0.00059890747 to 0.00059890747
- assignment: int32 [8], P('parts'), parts along dimension 0, may hold values from 0 to 3, each once
- padding: int32 [8], P(('parts', 'wide')), parts along dimension 0, may hold values from 0 to 1023
Outputs:
- scores: float32 [8, 1280], P(('parts', 'wide'), ('rep', 'sub')), parts along dimension 0
There are 2 independent parts, one for each index of `parts`. A program takes and returns all parts, laid end to end along the dimension named above; an argument that names none is the same for every part. Nothing has to cross between parts.
Inputs may be any that keep to these rules, and one draw needn't show every extreme that they name: `act_factor`: symmetric and positive definite. `delta_factor`: symmetric and positive definite. `assignment`: each number once.
All inputs are finite; a program needn't handle non-finite values.
Results may differ from a plain program's by a relative error of at most 0.005.
Values may be sent and summed in bfloat16 or wider, within the bound.
No kernel may reach another device: no remote copies, remote signals or barrier semaphores. Data moves between devices by JAX's collectives and lax.ppermute only.
A program may use at most 128 MiB of HBM per device.

v0:
```python
import jax
import jax.numpy as jnp
from jax import lax
from jax.sharding import PartitionSpec as P


def shards(activations, deltas, act_factor, delta_factor, queries, assignment, padding):
    seq_dev, tok_dev, feature_width = activations.shape
    full_length = tok_dev * lax.axis_size("sub")
    token_start = lax.axis_index("sub") * tok_dev
    positions = token_start + lax.broadcasted_iota(jnp.int32, (seq_dev, tok_dev), 1)
    kept_mask = positions < (full_length - padding)[:, None]
    masked = jnp.where(kept_mask[:, :, None], deltas, jnp.zeros((), jnp.bfloat16))
    delta_proj = jnp.einsum(
        "stw,wi->sti", masked, delta_factor, preferred_element_type=jnp.float32
    ).astype(jnp.bfloat16)
    act_proj = jnp.einsum(
        "stw,wj->stj",
        activations,
        lax.all_gather(act_factor, "rep", axis=1, tiled=True),
        preferred_element_type=jnp.float32,
    ).astype(jnp.bfloat16)
    partial_value = jnp.einsum(
        "sti,stj->sij", delta_proj, act_proj, preferred_element_type=jnp.float32
    )
    summed = lax.psum_scatter(partial_value, "sub", scatter_dimension=2, tiled=True).astype(
        jnp.bfloat16
    )
    regrouped = lax.all_to_all(summed, "wide", split_axis=1, concat_axis=0, tiled=True)
    seq_total = regrouped.shape[0]
    grad_rows = regrouped.reshape(seq_total, -1)
    query_rows = queries.reshape(queries.shape[0], -1)
    partial_scores = lax.dot_general(
        grad_rows, query_rows, (((1,), (1,)), ((), ())), preferred_element_type=jnp.float32
    )
    inverse_order = (
        jnp.zeros((seq_total,), jnp.int32)
        .at[assignment]
        .set(jnp.arange(seq_total, dtype=jnp.int32))
    )
    ranked = jnp.take(partial_scores, inverse_order, axis=0)
    by_column = lax.psum_scatter(ranked, ("rep", "sub"), scatter_dimension=1, tiled=True)
    return lax.psum_scatter(by_column, "wide", scatter_dimension=0, tiled=True)


def solution(mesh):
    placed = (
        P(("parts", "wide"), "sub", None),
        P(("parts", "wide"), "sub", None),
        P(None, "rep"),
        P(None, "rep"),
        P(None, ("rep", "wide"), "sub"),
        P("parts"),
        P(("parts", "wide")),
    )
    return jax.shard_map(
        shards,
        mesh=mesh,
        in_specs=placed,
        out_specs=P(("parts", "wide"), ("rep", "sub")),
        check_vma=False,
    )
```

profile of v0, /device:TPU:0, one launch (start us, length us, event | category | flops | bytes accessed | tf_op | source)
XLA Modules:
  0.0 137.5 jit_solution(17364108124651924373)
XLA Ops:
  7.3 10.2 %all_gather.3 = bf16[512,512]{1,0:T(8,128)(2,1)S(1)} all-gather(bf16[512,256]{1,0:T(8,128)(2,1)} %param.9), channel_id=1, replica_groups=mesh['parts'=2,'wide'=4,'rep'=2,'sub'=2] {'rep'}, dimensions={1}, use_global_device_ids=true | all-gather | bytes 786432 | tf_op jit(solution)/shard_map/all_gather | solution.py:20
  17.5 1.8 %convolution_convert_fusion.1 = bf16[1024,256]{1,0:T(8,128)(2,1)S(1)} fusion(bf16[512,256]{1,0:T(8,128)(2,1)} %param.10, bf16[1,1024,512]{2,1,0:T(8,128)(2,1)} %param.8, pred[1024]{0:T(1024)(128)(4,1)S(1)} %add_compare_fusion), kind=kOutput, calls=%fused_computation.4 | convolution fusion | flops 269221888 | bytes 1836032 | tf_op jit(solution)/shard_map/stw,wi->sti/dot_general | solution.py:14
  19.2 1.8 %fusion.1 = f32[1,256,512]{2,1,0:T(8,128)} fusion(bf16[1024,256]{1,0:T(8,128)(2,1)S(1)} %convolution_convert_fusion.1, bf16[512,512]{1,0:T(8,128)(2,1)S(1)} %all_gather.3, bf16[1,1024,512]{2,1,0:T(8,128)(2,1)S(1)} %copy-done), kind=kOutput, calls=%fused_computation.5 | convolution fusion | flops 805830656 | bytes 2621440 | tf_op jit(solution)/shard_map/sti,stj->sij/dot_general | solution.py:23
  21.1 38.2 %copy.12 = bf16[160,8,64,256]{3,1,2,0:T(8,128)(2,1)} copy(bf16[160,8,64,256]{3,2,1,0:T(8,128)(2,1)} %bitcast.26) | data formatting | bytes 83886080
  59.3 0.6 scatter_custom_fusion
  59.9 1.0 convert_element_type.13
  60.9 0.2 copy.14
  61.1 0.5 broadcast.49
  61.6 1.4 %reduce.2 = bf16[256,256]{1,0:T(8,128)(2,1)S(1)} reduce(bf16[256,1,256]{2,1,0:T(2,128)(2,1)S(1)} %bitcast.28, bf16[]{:T(256)} %broadcast.49), dimensions={1}, to_apply=%bitcast.24.reduce_sub_computation | reduce | bytes 262146
  63.0 0.7 reshape.71
  63.7 5.1 %all-to-all-start = ((bf16[4,2,8192]{2,1,0:T(2,128)(2,1)}), bf16[4,2,8192]{2,1,0:T(2,128)(2,1)S(1)}, u32[]{:S(2)}, u32[]{:S(2)}) async-start(bf16[4,2,8192]{2,1,0:T(2,128)(2,1)} %reshape.71), calls=%async_computation.1 | async-start | bytes 262144 | tf_op jit(solution)/shard_map/all_to_all | solution.py:29
  68.8 5.9 %all-to-all-done = bf16[4,2,8192]{2,1,0:T(2,128)(2,1)S(1)} async-done(((bf16[4,2,8192]{2,1,0:T(2,128)(2,1)}), bf16[4,2,8192]{2,1,0:T(2,128)(2,1)S(1)}, u32[]{:S(2)}, u32[]{:S(2)}) %all-to-all-start) | async-done | bytes 131104 | tf_op jit(solution)/shard_map/all_to_all | solution.py:29
  74.7 0.1 reshape.72
  74.8 0.7 bitcast_reduce_fusion
  75.6 0.1 reshape.45
  75.7 17.5 %fusion.11 = f32[4,1280]{1,0:T(4,128)S(1)} fusion(bf16[4,16384]{1,0:T(4,128)(2,1)S(1)} %reshape.45, bf16[1280,16384]{1,0:T(8,128)(2,1)} %bitcast.25), kind=kOutput, calls=%fused_computation.23 | convolution fusion | flops 167772160 | bytes 42094592 | tf_op jit(solution)/shard_map/dot_general | solution.py:33
  93.2 0.6 gather_fusion
  93.7 0.1 broadcast_select_fusion
  93.8 1.1 copy.10
  95.0 0.6 dynamic-slice
  95.6 21.1 %reduce-scatter.7.cloned.1.call-done = f32[320,4]{1,0:T(8,128)} async-done(((f32[1280,4]{1,0:T(8,128)}), f32[320,4]{1,0:T(8,128)}) %reduce-scatter.7.cloned.1.call-update) | async-done | bytes 5136
  116.6 1.0 copy.11
  117.6 11.8 %all-reduce = f32[4,320]{1,0:T(4,128)S(1)} all-reduce(f32[4,320]{1,0:T(4,128)S(1)} %copy.11), channel_id=4, replica_groups=mesh['parts'=2,'wide'=4,'rep'=2,'sub'=2] {'wide'}, use_global_device_ids=true, to_apply=%region_3.4.clone | all-reduce | flops 1280 | bytes 10240
  129.5 1.2 constant_dynamic-slice_fusion
  (19 shorter events, 0.1 us)
Async XLA Ops:
  6.5 12.7 %copy-start = (bf16[1,1024,512]{2,1,0:T(8,128)(2,1)S(1)}, bf16[1,1024,512]{2,1,0:T(8,128)(2,1)}, u32[]{:S(2)}) copy-start(bf16[1,1024,512]{2,1,0:T(8,128)(2,1)} %param.7) | copy-start | bytes 3145732
  6.5 53.4 %reduce-scatter.5.cloned.1.call-start = ((), (), s32[]{:S(2)}) async-start(), calls=%async_computation.3 | async-start | bytes 786432 | tf_op jit(solution)/shard_map/reduce_scatter | solution.py:26
  21.0 38.2 %copy-start.2 = (s32[4]{0:T(128)S(1)}, s32[4]{0:T(128)}, u32[]{:S(2)}) copy-start(s32[4]{0:T(128)} %param.12) | copy-start | bytes 52
  21.1 109.6 %copy-start.1 = (bf16[1,1024,512]{2,1,0:T(8,128)(2,1)S(1)}, bf16[1,1024,512]{2,1,0:T(8,128)(2,1)}, u32[]{:S(2)}) copy-start(bf16[1,1024,512]{2,1,0:T(8,128)(2,1)} %param.7) | copy-start | bytes 3145732
  59.2 35.7 %copy-start.3 = (u32[32]{0:T(128)S(1)}, u32[32]{0:T(128)}, u32[]{:S(2)}) copy-start(u32[32]{0:T(128)} %constant.33) | copy-start | bytes 388
  63.7 11.0 %all-to-all-start = ((bf16[4,2,8192]{2,1,0:T(2,128)(2,1)}), bf16[4,2,8192]{2,1,0:T(2,128)(2,1)S(1)}, u32[]{:S(2)}, u32[]{:S(2)}) async-start(bf16[4,2,8192]{2,1,0:T(2,128)(2,1)} %reshape.71), calls=%async_computation.1 | async-start | bytes 262144 | tf_op jit(solution)/shard_map/all_to_all | solution.py:29
  68.8 47.9 %reduce-scatter.7.cloned.1.call-start = ((), (), s32[]{:S(2)}) async-start(), calls=%async_computation.4 | async-start | bytes 819200
Sparse Core Ops, SparseCore 0:
  21.2 9.4 reduce-scatter.4
  95.1 21.5 reduce-scatter.6
where the time goes:
time: 138 us
  local copies, waits for them, and re-layouts  45.6 us (33%)
  waiting for transfers between devices  27 us (20%)
  blocking collectives  22 us (16%)
  matrix products  21 us (15%)
  between operations  14.3 us (10%)
  starting transfers between devices  5.09 us (4%)
  other arithmetic  2.47 us (2%)
    unnamed x16, local copies, waits for them, and re-layouts  43.4 us
    unnamed x3, waiting for transfers between devices  21.1 us
    dot_general x1, matrix products, shards(): lax.dot_general(grad_rows, query_rows, (((1,), (1,)), ((), ())), preferre...  17.5 us
    unnamed x1, blocking collectives  11.8 us
    all_gather x1, blocking collectives, shards(): lax.all_gather(act_factor, 'rep', axis=1, tiled=True)  10.2 us
    all_to_all x1, waiting for transfers between devices, shards(): lax.all_to_all(summed, 'wide', split_axis=1, concat_axis=0, tiled=True)  5.91 us
    all_to_all x1, starting transfers between devices, shards(): lax.all_to_all(summed, 'wide', split_axis=1, concat_axis=0, tiled=True)  5.08 us
  transfers between devices with their start and end apart: 3, of which 2 were waited for; matrix products, arithmetic and copies ran while one was open for 29% of the time, Pallas kernels for 0%

commit v1 on v0

v1 whole, which is shorter than its diff:
```python
import functools

import jax
import jax.numpy as jnp
from jax import lax
from jax.experimental import pallas as pl
from jax.experimental.pallas import tpu as pltpu
from jax.sharding import PartitionSpec as P

GROUP = 16
F32 = jnp.float32
BF16 = jnp.bfloat16
NT = (((1,), (1,)), ((), ()))
TN = (((0,), (0,)), ((), ()))


def row_product_kernel(token_steps, pad_ref, deltas_ref, acts_ref, factor_ref, out_ref):
    step = pl.program_id(0)
    tokens = deltas_ref.shape[0]
    first = (lax.axis_index("sub") * token_steps + step) * tokens
    limit = lax.axis_size("sub") * token_steps * tokens - pad_ref[0]
    position = first + lax.broadcasted_iota(jnp.int32, (tokens, 1), 0)
    masked = jnp.where(position < limit, deltas_ref[...], jnp.zeros((), BF16))
    proj = jnp.dot(masked, factor_ref[...], preferred_element_type=F32).astype(BF16)
    term = lax.dot_general(proj, acts_ref[...], TN, preferred_element_type=F32)

    @pl.when(step == 0)
    def _():
        out_ref[...] = term

    @pl.when(step > 0)
    def _():
        out_ref[...] += term


def row_product(padding, deltas, acts, factor):
    tokens, width = deltas.shape
    rows = factor.shape[1]
    steps = 4 if tokens % 1024 == 0 else 1
    block = tokens // steps
    return pl.pallas_call(
        functools.partial(row_product_kernel, steps),
        grid=(steps,),
        out_shape=jax.ShapeDtypeStruct((rows, width), F32),
        in_specs=[
            pl.BlockSpec(memory_space=pltpu.SMEM),
            pl.BlockSpec((block, width), lambda i: (i, 0)),
            pl.BlockSpec((block, width), lambda i: (i, 0)),
            pl.BlockSpec((width, rows), lambda i: (0, 0)),
        ],
        out_specs=pl.BlockSpec((rows, width), lambda i: (0, 0)),
        compiler_params=pltpu.CompilerParams(vmem_limit_bytes=12 << 20),
        cost_estimate=pl.CostEstimate(
            flops=4 * tokens * width * rows, bytes_accessed=4 * tokens * width, transcendentals=0
        ),
    )(padding, deltas, acts, factor)


def grad_kernel(parts, wide, seq_ref, mine_ref, other_ref, factor_ref, far_ref, out_ref):
    rep, sub = lax.axis_index("rep"), lax.axis_index("sub")
    half = factor_ref.shape[1]
    rows = mine_ref.shape[0] // (parts * wide)
    summed = mine_ref[...] + other_ref[...]
    high = summed.astype(BF16)
    low = (summed - high.astype(F32)).astype(BF16)

    def emit(grad):
        tag = lax.broadcasted_iota(jnp.int32, (GROUP, half), 1) == seq_ref[0]
        for part in range(parts):
            for place in range(wide):
                block = part * wide + place
                start = (place * parts + part) * rows
                out_ref[block, :rows, :] = grad[start : start + rows].astype(BF16)
                out_ref[block, rows:, :] = tag.astype(F32).astype(BF16)

    def product(values, near, far, near_rows):
        first, second = values[:, :half], values[:, half:]
        if near_rows == 0:
            a, b = first, second
        else:
            a, b = second, first
        return lax.dot_general(a, near, NT, preferred_element_type=F32) + jnp.dot(
            b, far, preferred_element_type=F32
        )

    @pl.when(rep == sub)
    def _():
        whole = factor_ref[...]
        emit(
            jnp.dot(high, whole, preferred_element_type=F32)
            + jnp.dot(low, whole, preferred_element_type=F32)
        )

    for index in range(2):

        @pl.when((rep != sub) & (rep == index))
        def _():
            other = 1 - index
            near = factor_ref[other * half : (other + 1) * half, :]
            far = far_ref[...]
            emit(product(high, near, far, index) + product(low, near, far, index))


def grad_blocks(parts, wide, seq, mine, other, factor, far):
    rows, width = mine.shape
    block = rows // (parts * wide)
    half = factor.shape[1]
    vmem = pl.BlockSpec(memory_space=pltpu.VMEM)
    return pl.pallas_call(
        functools.partial(grad_kernel, parts, wide),
        out_shape=jax.ShapeDtypeStruct((parts * wide, block + GROUP, half), BF16),
        in_specs=[pl.BlockSpec(memory_space=pltpu.SMEM)] + [vmem] * 4,
        out_specs=vmem,
        compiler_params=pltpu.CompilerParams(vmem_limit_bytes=12 << 20),
        cost_estimate=pl.CostEstimate(
            flops=4 * rows * width * half, bytes_accessed=12 * rows * width, transcendentals=0
        ),
    )(seq, mine, other, factor, far)


def score_kernel(blocks, pieces, grads_ref, queries_ref, out_ref, held, sems):
    seqs, padded, width = grads_ref.shape
    rows = padded - GROUP
    total = queries_ref.shape[0]
    piece = total // pieces
    start = pl.multiple_of(lax.axis_index("parts") * rows, rows)

    def copy(i):
        return pltpu.make_async_copy(
            queries_ref.at[pl.ds(i * piece, piece), pl.ds(start, rows), :],
            held.at[pl.ds(i * piece, piece)],
            sems.at[i],
        )

    for i in range(pieces):
        copy(i).start()

    lanes = seqs * GROUP
    weights = jnp.concatenate(
        [
            grads_ref[:, g : g + GROUP, :].reshape(lanes, width)
            for g in range(0, rows, GROUP)
        ],
        axis=1,
    )
    lane = lax.broadcasted_iota(jnp.int32, (GROUP, lanes), 1)
    diagonal = lax.broadcasted_iota(jnp.int32, (GROUP, lanes), 0) == lane % GROUP
    tags = grads_ref[:, rows, :]
    owner = lax.broadcasted_iota(jnp.int32, (seqs, lanes), 0) == (
        lax.broadcasted_iota(jnp.int32, (seqs, lanes), 1) // GROUP
    )
    place = lax.dot_general(
        tags, owner.astype(F32).astype(BF16), TN, preferred_element_type=F32
    )[:seqs]

    per_block = total // blocks
    sub_pieces = pieces // blocks
    for block in range(blocks):
        sums = []
        for j in range(sub_pieces):
            i = block * sub_pieces + j
            copy(i).wait()
            at = pl.ds(i * piece, piece)
            rows_of = jnp.concatenate(
                [
                    held[at, g : g + GROUP, :].reshape(piece * GROUP, width)
                    for g in range(0, rows, GROUP)
                ],
                axis=1,
            )
            found = lax.dot_general(rows_of, weights, NT, preferred_element_type=F32)
            kept = jnp.where(diagonal, found.reshape(piece, GROUP, lanes), 0.0)
            sums.append(jnp.sum(kept, axis=1))
        by_query = sums[0] if len(sums) == 1 else jnp.concatenate(sums, axis=0)
        scores = lax.dot_general(
            place, by_query, NT, preferred_element_type=F32, precision=lax.Precision.HIGHEST
        )
        for m in range(seqs):
            out_ref[m * blocks + block] = scores[m : m + 1]


def score_blocks(blocks, grads, queries):
    seqs, padded, width = grads.shape
    rows = padded - GROUP
    total = queries.shape[0]
    pieces = blocks * 2
    return pl.pallas_call(
        functools.partial(score_kernel, blocks, pieces),
        out_shape=jax.ShapeDtypeStruct((seqs * blocks, 1, total // blocks), F32),
        in_specs=[pl.BlockSpec(memory_space=pltpu.VMEM), pl.BlockSpec(memory_space=pl.ANY)],
        out_specs=pl.BlockSpec(memory_space=pltpu.VMEM),
        scratch_shapes=[
            pltpu.VMEM((total, rows, width), BF16),
            pltpu.SemaphoreType.DMA((pieces,)),
        ],
        compiler_params=pltpu.CompilerParams(vmem_limit_bytes=48 << 20),
        cost_estimate=pl.CostEstimate(
            flops=2 * total * rows * width * 128,
            bytes_accessed=2 * total * rows * width,
            transcendentals=0,
        ),
    )(grads, queries)


def shared(activations, deltas, act_factor, delta_factor, queries, assignment, padding):
    parts, wide = lax.axis_size("parts"), lax.axis_size("wide")
    rep, sub = lax.axis_size("rep"), lax.axis_size("sub")
    half = act_factor.shape[1]
    own_block = lax.dynamic_slice_in_dim(act_factor, lax.axis_index("rep") * half, half, axis=0)
    far_block = lax.ppermute(own_block, "rep", [(0, 1), (1, 0)])
    mine = row_product(padding, deltas[0], activations[0], delta_factor)
    other = lax.ppermute(mine, "sub", [(0, 1), (1, 0)])
    seq = assignment[lax.axis_index("wide")] + lax.axis_index("parts") * wide
    sent = grad_blocks(parts, wide, seq[None], mine, other, act_factor, far_block)
    grads = lax.all_to_all(sent, ("parts", "wide"), split_axis=0, concat_axis=0, tiled=True)
    partial = score_blocks(rep * sub, grads, queries)
    gathered = lax.all_to_all(
        partial, ("parts", "wide", "rep", "sub"), split_axis=0, concat_axis=0, tiled=True
    )
    return jnp.sum(gathered, axis=0)


def general(activations, deltas, act_factor, delta_factor, queries, assignment, padding):
    seq_dev, tok_dev, _ = activations.shape
    full_length = tok_dev * lax.axis_size("sub")
    token_start = lax.axis_index("sub") * tok_dev
    positions = token_start + lax.broadcasted_iota(jnp.int32, (seq_dev, tok_dev), 1)
    kept_mask = positions < (full_length - padding)[:, None]
    masked = jnp.where(kept_mask[:, :, None], deltas, jnp.zeros((), BF16))
    delta_proj = jnp.einsum(
        "stw,wi->sti", masked, delta_factor, preferred_element_type=F32
    ).astype(BF16)
    act_proj = jnp.einsum(
        "stw,wj->stj",
        activations,
        lax.all_gather(act_factor, "rep", axis=1, tiled=True),
        preferred_element_type=F32,
    ).astype(BF16)
    partial_value = jnp.einsum("sti,stj->sij", delta_proj, act_proj, preferred_element_type=F32)
    summed = lax.psum_scatter(partial_value, "sub", scatter_dimension=2, tiled=True).astype(BF16)
    regrouped = lax.all_to_all(summed, "wide", split_axis=1, concat_axis=0, tiled=True)
    seq_total = regrouped.shape[0]
    grad_rows = regrouped.reshape(seq_total, -1)
    query_rows = queries.reshape(queries.shape[0], -1)
    partial_scores = lax.dot_general(grad_rows, query_rows, NT, preferred_element_type=F32)
    inverse_order = (
        jnp.zeros((seq_total,), jnp.int32)
        .at[assignment]
        .set(jnp.arange(seq_total, dtype=jnp.int32))
    )
    ranked = jnp.take(partial_scores, inverse_order, axis=0)
    by_column = lax.psum_scatter(ranked, ("rep", "sub"), scatter_dimension=1, tiled=True)
    return lax.psum_scatter(by_column, "wide", scatter_dimension=0, tiled=True)


def shards(activations, deltas, act_factor, delta_factor, queries, assignment, padding):
    parts, wide = lax.axis_size("parts"), lax.axis_size("wide")
    rep, sub = lax.axis_size("rep"), lax.axis_size("sub")
    fits = (
        rep == 2
        and sub == 2
        and activations.shape[0] == 1
        and queries.shape[1] % (parts * GROUP) == 0
        and parts * wide * GROUP <= 128
        and queries.shape[0] % (2 * rep * sub) == 0
        and act_factor.shape[1] % 128 == 0
    )
    body = shared if fits else general
    return body(activations, deltas, act_factor, delta_factor, queries, assignment, padding)


def solution(mesh):
    placed = (
        P(("parts", "wide"), "sub", None),
        P(("parts", "wide"), "sub", None),
        P(None, "rep"),
        P(None, "rep"),
        P(None, ("rep", "wide"), "sub"),
        P("parts"),
        P(("parts", "wide")),
    )
    return jax.shard_map(
        shards,
        mesh=mesh,
        in_specs=placed,
        out_specs=P(("parts", "wide"), ("rep", "sub")),
        check_vma=False,
    )
```

time: 138 us -> 55.4 us (0.40)
  local copies, waits for them, and re-layouts: 45.6 us -> 7.06 us
  waiting for transfers between devices: 27 us -> 2.26 us
  matrix products: 21 us -> 0 us
  Pallas kernels: 0 us -> 17.7 us
  between operations: 14.3 us -> 1.35 us
  other arithmetic: 2.47 us -> 0.06 us
  starting transfers between devices: 5.09 us -> 3.09 us
  blocking collectives: 22 us -> 23.5 us
    unnamed x16 -> x8, local copies, waits for them, and re-layouts: 43.4 us -> 4.34 us
    all_to_all x0 -> x2, blocking collectives: none -> 23.5 us  [the longest x1 14.5 us: shared(): lax.all_to_all(sent, ('parts', 'wide'), split_axis=0, concat_axis=0, tile...]
    unnamed x3 -> x0, waiting for transfers between devices: 21.1 us -> none
    dot_general x3 -> x0, matrix products: 21 us -> none  [the longest x1 17.5 us: shards(): lax.dot_general(grad_rows, query_rows, (((1,), (1,)), ((), ())), preferre...]
    pallas_call x0 -> x3, Pallas kernels: none -> 17.7 us  [the longest x1 14.8 us: score_blocks(): pl.pallas_call(functools.partial(score_kernel, blocks, pieces), out_shape...]
    unnamed x1 -> x0, blocking collectives: 11.8 us -> none
    all_gather x1 -> x0, blocking collectives: 10.2 us -> none  [shards(): lax.all_gather(act_factor, 'rep', axis=1, tiled=True)]
    all_to_all x1 -> x0, waiting for transfers between devices: 5.91 us -> none  [shards(): lax.all_to_all(summed, 'wide', split_axis=1, concat_axis=0, tiled=True)]
  transfers between devices with their start and end apart: 3 -> 2, of which waited for: 2 -> 1; matrix products, arithmetic and copies ran while one was open for 29% -> 4% of each run, Pallas kernels for 0% -> 0%
where the time goes in v1:
time: 55.4 us; the launch traced here: 55 us
  blocking collectives  23.5 us (42%)
  Pallas kernels  17.7 us (32%)
  local copies, waits for them, and re-layouts  7.06 us (13%)
  starting transfers between devices  3.09 us (6%)
  waiting for transfers between devices  2.26 us (4%)
  between operations  1.35 us (2%)
    pallas_call x1, Pallas kernels, score_blocks(): pl.pallas_call(functools.partial(score_kernel, blocks, pieces), out_shape...  14.8 us
    all_to_all x1, blocking collectives, shared(): lax.all_to_all(sent, ('parts', 'wide'), split_axis=0, concat_axis=0, tile...  14.5 us
    all_to_all x1, blocking collectives, shared(): lax.all_to_all(partial, ('parts', 'wide', 'rep', 'sub'), split_axis=0, co...  9.03 us
    unnamed x8, local copies, waits for them, and re-layouts  4.34 us
    ppermute x1, starting transfers between devices, shared(): far_block = lax.ppermute(own_block, 'rep', [(0, 1), (1, 0)])  2.58 us
    pallas_call x1, Pallas kernels, row_product(): pl.pallas_call(functools.partial(row_product_kernel, steps), grid=(steps,...  2.46 us
    ppermute x1, waiting for transfers between devices, shared(): far_block = lax.ppermute(own_block, 'rep', [(0, 1), (1, 0)])  2.26 us
    dynamic_slice x1, local copies, waits for them, and re-layouts, shared(): seq = assignment[lax.axis_index('wide')] + lax.axis_index('parts') * wide  1.24 us
  transfers between devices with their start and end apart: 2, of which 1 were waited for; matrix products, arithmetic and copies ran while one was open for 4% of the time, Pallas kernels for 0%

profile of v1, /device:TPU:0, one launch (start us, length us, event | category | flops | bytes accessed | tf_op | source)
XLA Modules:
  0.0 55.0 jit_solution(16621129681745054364)
XLA Ops:
  0.7 0.0 copy-start
  0.7 1.2 %copy-done = bf16[1,1024,512]{2,1,0:T(8,128)(2,1)S(1)} copy-done((bf16[1,1024,512]{2,1,0:T(8,128)(2,1)S(1)}, bf16[1,1024,512]{2,1,0:T(8,128)(2,1)}, u32[]{:S(2)}) %copy-start) | copy-done | bytes 1048600
  1.9 0.0 copy-start.1
  1.9 1.2 %copy-done.1 = bf16[1,1024,512]{2,1,0:T(8,128)(2,1)S(1)} copy-done((bf16[1,1024,512]{2,1,0:T(8,128)(2,1)S(1)}, bf16[1,1024,512]{2,1,0:T(8,128)(2,1)}, u32[]{:S(2)}) %copy-start.1) | copy-done | bytes 1048600
  3.1 0.0 copy-start.3
  3.1 0.9 %copy-done.3 = bf16[512,256]{1,0:T(8,128)(2,1)S(1)} copy-done((bf16[512,256]{1,0:T(8,128)(2,1)S(1)}, bf16[512,256]{1,0:T(8,128)(2,1)}, u32[]{:S(2)}) %copy-start.3) | copy-done | bytes 262168
  4.1 2.5 %shard_map.73.mine_ref = f32[256,512]{1,0:T(8,128)S(1)} custom-call(s32[1]{0:T(128)S(6)} %copy.8.pad_ref, bf16[1024,512]{1,0:T(8,128)(2,1)S(1)} %bitcast.4, bf16[1024,512]{1,0:T(8,128)(2,1)S(1)} %bitcast.5, bf16[512,256]{1,0:T(8,128)(2,1)S(1)} %copy-done.3), custom_call_target="tpu_custom_call" | custom-call | flops 536870912 | bytes 2097152 | tf_op jit(solution)/shard_map/pallas_call | solution.py:41
  6.5 0.5 collective-permute-start
  7.0 0.9 %constant_dynamic-slice_fusion = bf16[256,256]{1,0:T(8,128)(2,1)S(1)} fusion(bf16[512,256]{1,0:T(8,128)(2,1)} %factor_ref.3, s32[]{:T(128)S(6)} %select_n.7), kind=kLoop, calls=%fused_computation | loop fusion | bytes 262148 | tf_op jit(solution)/shard_map/dynamic_slice | solution.py:209
  8.0 2.6 %collective-permute-start.1 = (bf16[256,256]{1,0:T(8,128)(2,1)S(1)}, bf16[256,256]{1,0:T(8,128)(2,1)S(1)}, u32[]{:S(2)}, u32[]{:S(2)}) collective-permute-start(bf16[256,256]{1,0:T(8,128)(2,1)S(1)} %constant_dynamic-slice_fusion), channel_id=1, source_target_pairs={{0,2},{2,0},{1,3},{3,1},{4,6},{6,4},{5,7},{7,5},{8,10},{10,8},{9,1... | collective-permute-start | bytes 393224 | tf_op jit(solution)/shard_map/ppermute | solution.py:210
  10.5 1.2 %dynamic_slice.6 = s32[1]{0:T(128)} dynamic-slice(s32[4]{0:T(128)} %param.12, s32[]{:T(128)S(6)} %select_n.6), dynamic_slice_sizes={1} | dynamic-slice | bytes 12 | tf_op jit(solution)/shard_map/dynamic_slice | solution.py:213
  12.4 2.3 %collective-permute-done.1.far_ref = bf16[256,256]{1,0:T(8,128)(2,1)S(1)} collective-permute-done((bf16[256,256]{1,0:T(8,128)(2,1)S(1)}, bf16[256,256]{1,0:T(8,128)(2,1)S(1)}, u32[]{:S(2)}, u32[]{:S(2)}) %collective-permute-start.1) | collective-permute-done | bytes 131104 | tf_op jit(solution)/shard_map/ppermute | solution.py:210
  14.7 0.0 collective-permute-done.other_ref
  14.7 0.0 copy-start.2
  14.7 0.9 %copy-done.2 = bf16[512,256]{1,0:T(8,128)(2,1)S(1)} copy-done((bf16[512,256]{1,0:T(8,128)(2,1)S(1)}, bf16[512,256]{1,0:T(8,128)(2,1)}, u32[]{:S(2)}) %copy-start.2) | copy-done | bytes 262168
  15.6 0.4 shard_map.74
  16.1 14.5 %all_to_all.10.grads_ref = bf16[8,48,256]{2,1,0:T(8,128)(2,1)S(1)} all-to-all(bf16[8,48,256]{2,1,0:T(8,128)(2,1)S(1)} %shard_map.74), channel_id=1, replica_groups=mesh['parts'=2,'wide'=4,'rep'=2,'sub'=2] {'parts','wide'}, dimensions={0} | all-to-all | bytes 393216 | tf_op jit(solution)/shard_map/all_to_all | solution.py:215
  30.6 14.8 %shard_map.75 = f32[32,1,320]{2,1,0:T(1,128)S(1)} custom-call(bf16[8,48,256]{2,1,0:T(8,128)(2,1)S(1)} %all_to_all.10.grads_ref, bf16[1280,64,256]{2,1,0:T(8,128)(2,1)} %queries_ref.1), custom_call_target="tpu_custom_call" | custom-call | flops 2684354560 | bytes 20971520 | tf_op jit(solution)/shard_map/pallas_call | solution.py:187
  45.4 9.0 %all_to_all.11 = f32[32,1,320]{2,1,0:T(1,128)S(1)} all-to-all(f32[32,1,320]{2,1,0:T(1,128)S(1)} %shard_map.75), channel_id=1, replica_groups=mesh['parts'=2,'wide'=4,'rep'=2,'sub'=2] {'parts','wide','rep','sub'}, dimensions={0} | all-to-all | bytes 81920 | tf_op jit(solution)/shard_map/all_to_all | solution.py:217
  54.4 0.1 reduce_sum.11
  54.4 0.6 %reduce_sum.12 = f32[1,320]{1,0:T(1,128)} reshape(f32[320]{0:T(512)S(1)} %reduce_sum.11) | data formatting | bytes 2560 | tf_op jit(solution)/shard_map/reduce_sum | solution.py:220
Async XLA Ops:
  0.7 1.2 %copy-start = (bf16[1,1024,512]{2,1,0:T(8,128)(2,1)S(1)}, bf16[1,1024,512]{2,1,0:T(8,128)(2,1)}, u32[]{:S(2)}) copy-start(bf16[1,1024,512]{2,1,0:T(8,128)(2,1)} %param.8) | copy-start | bytes 3145732
  1.9 1.2 %copy-start.1 = (bf16[1,1024,512]{2,1,0:T(8,128)(2,1)S(1)}, bf16[1,1024,512]{2,1,0:T(8,128)(2,1)}, u32[]{:S(2)}) copy-start(bf16[1,1024,512]{2,1,0:T(8,128)(2,1)} %param.7) | copy-start | bytes 3145732
  3.1 0.9 %copy-start.3 = (bf16[512,256]{1,0:T(8,128)(2,1)S(1)}, bf16[512,256]{1,0:T(8,128)(2,1)}, u32[]{:S(2)}) copy-start(bf16[512,256]{1,0:T(8,128)(2,1)} %factor_ref.2) | copy-start | bytes 786436
  6.5 8.2 %collective-permute-start = (f32[256,512]{1,0:T(8,128)S(1)}, f32[256,512]{1,0:T(8,128)S(1)}, u32[]{:S(2)}, u32[]{:S(2)}) collective-permute-start(f32[256,512]{1,0:T(8,128)S(1)} %shard_map.73.mine_ref), channel_id=1, source_target_pairs={{0,1},{1,0},{2,3},{3,2},{4,5},{5,4},{6,7},{7,6},{8,9},{9,8},{10,11... | collective-permute-start | bytes 1572872 | tf_op jit(solution)/shard_map/ppermute | solution.py:212
  8.0 6.7 %collective-permute-start.1 = (bf16[256,256]{1,0:T(8,128)(2,1)S(1)}, bf16[256,256]{1,0:T(8,128)(2,1)S(1)}, u32[]{:S(2)}, u32[]{:S(2)}) collective-permute-start(bf16[256,256]{1,0:T(8,128)(2,1)S(1)} %constant_dynamic-slice_fusion), channel_id=1, source_target_pairs={{0,2},{2,0},{1,3},{3,1},{4,6},{6,4},{5,7},{7,5},{8,10},{10,8},{9,1... | collective-permute-start | bytes 393224 | tf_op jit(solution)/shard_map/ppermute | solution.py:210
  14.7 1.0 %copy-start.2 = (bf16[512,256]{1,0:T(8,128)(2,1)S(1)}, bf16[512,256]{1,0:T(8,128)(2,1)}, u32[]{:S(2)}) copy-start(bf16[512,256]{1,0:T(8,128)(2,1)} %factor_ref.3) | copy-start | bytes 786436

commit v2 on v0

v2 whole, which is shorter than its diff:
```python
import functools

import jax
import jax.numpy as jnp
from jax import lax
from jax.experimental import pallas as pl
from jax.experimental.pallas import tpu as pltpu
from jax.sharding import PartitionSpec as P

GROUP = 16
F32 = jnp.float32
BF16 = jnp.bfloat16
NT = (((1,), (1,)), ((), ()))
TN = (((0,), (0,)), ((), ()))


def row_product_kernel(
    pad_ref, deltas_ref, acts_ref, row_factor_ref, col_factor_ref, queries_ref,
    out_ref, col_out_ref, early_ref,
    pad_in, deltas_in, acts_in, factor_in, sems,
):
    steps, tokens, _ = deltas_in.shape
    first = lax.axis_index("sub") * steps * tokens

    def copy(source, held, which, i):
        return pltpu.make_async_copy(
            source.at[pl.ds(i * tokens, tokens), :], held.at[i], sems.at[which, i]
        )

    row_copy = pltpu.make_async_copy(row_factor_ref, factor_in, sems.at[2, 0])
    col_copy = pltpu.make_async_copy(col_factor_ref, col_out_ref, sems.at[2, 1])
    pad_copy = pltpu.make_async_copy(pad_ref, pad_in, sems.at[2, 2])
    pad_copy.start()
    row_copy.start()
    for i in range(steps):
        copy(deltas_ref, deltas_in, 0, i).start()
        copy(acts_ref, acts_in, 1, i).start()
    col_copy.start()
    early_copy = pltpu.make_async_copy(
        queries_ref.at[pl.ds(0, early_ref.shape[0])], early_ref, sems.at[2, 3]
    )
    early_copy.start()
    out_ref[...] = jnp.zeros(out_ref.shape, F32)
    pad_copy.wait()
    row_copy.wait()
    limit = lax.axis_size("sub") * steps * tokens - pad_in[0]

    def step(i, carry):
        copy(deltas_ref, deltas_in, 0, i).wait()
        copy(acts_ref, acts_in, 1, i).wait()
        position = first + i * tokens + lax.broadcasted_iota(jnp.int32, (tokens, 1), 0)
        masked = jnp.where(position < limit, deltas_in[i], jnp.zeros((), BF16))
        proj = jnp.dot(masked, factor_in[...], preferred_element_type=F32).astype(BF16)
        out_ref[...] += lax.dot_general(proj, acts_in[i], TN, preferred_element_type=F32)
        return carry

    lax.fori_loop(0, steps, step, 0)
    col_copy.wait()
    early_copy.wait()


def row_product(padding, deltas, acts, row_factor, col_factor, queries, early):
    tokens, width = deltas.shape
    rows = row_factor.shape[1]
    steps = max(1, tokens // 512)
    hbm = pl.BlockSpec(memory_space=pltpu.HBM)
    vmem = pl.BlockSpec(memory_space=pltpu.VMEM)
    operands = [padding] + [
        pltpu.with_memory_space_constraint(x, pltpu.HBM)
        for x in (deltas, acts, row_factor, col_factor, queries)
    ]
    return pl.pallas_call(
        row_product_kernel,
        out_shape=(
            jax.ShapeDtypeStruct((rows, width), F32),
            jax.ShapeDtypeStruct(col_factor.shape, BF16),
            pltpu.VMEM((early,) + queries.shape[1:], BF16),
        ),
        in_specs=[pl.BlockSpec(memory_space=pl.ANY)] + [hbm] * 5,
        out_specs=(vmem, vmem, vmem),
        scratch_shapes=[
            pltpu.SMEM(padding.shape, jnp.int32),
            pltpu.VMEM((steps, tokens // steps, width), BF16),
            pltpu.VMEM((steps, tokens // steps, width), BF16),
            pltpu.VMEM(row_factor.shape, BF16),
            pltpu.SemaphoreType.DMA((3, max(4, steps))),
        ],
        compiler_params=pltpu.CompilerParams(vmem_limit_bytes=12 << 20),
        cost_estimate=pl.CostEstimate(
            flops=4 * tokens * width * rows, bytes_accessed=4 * tokens * width, transcendentals=0
        ),
    )(*operands)


def grad_kernel(wide, mine_ref, other_ref, factor_ref, far_ref, *outs_and_scratch):
    *outs, held = outs_and_scratch
    rep, sub, place = (lax.axis_index(a) for a in ("rep", "sub", "wide"))
    half = factor_ref.shape[1]
    rows = mine_ref.shape[0] // wide
    summed = mine_ref[...] + other_ref[...]
    high = summed.astype(BF16)
    low = (summed - high.astype(F32)).astype(BF16)

    @pl.when(rep == sub)
    def _():
        whole = factor_ref[...]
        held[...] = jnp.dot(high, whole, preferred_element_type=F32) + jnp.dot(
            low, whole, preferred_element_type=F32
        )

    for index in range(2):

        @pl.when((rep != sub) & (rep == index))
        def _():
            here = slice(index * half, (index + 1) * half)
            there = slice((1 - index) * half, (2 - index) * half)
            near, far = factor_ref[there, :], far_ref[...]
            held[...] = (
                lax.dot_general(high[:, here], near, NT, preferred_element_type=F32)
                + lax.dot_general(low[:, here], near, NT, preferred_element_type=F32)
                + jnp.dot(high[:, there], far, preferred_element_type=F32)
                + jnp.dot(low[:, there], far, preferred_element_type=F32)
            )

    for k in range(wide):
        start = pl.multiple_of((place ^ k) * rows, rows)
        outs[k][...] = held[pl.ds(start, rows), :].astype(BF16)


def grad_blocks(wide, mine, other, factor, far):
    rows, width = mine.shape
    half = factor.shape[1]
    vmem = pl.BlockSpec(memory_space=pltpu.VMEM)
    return pl.pallas_call(
        functools.partial(grad_kernel, wide),
        out_shape=[jax.ShapeDtypeStruct((rows // wide, half), BF16)] * wide,
        in_specs=[vmem] * 4,
        out_specs=[vmem] * wide,
        scratch_shapes=[pltpu.VMEM((rows, half), F32)],
        compiler_params=pltpu.CompilerParams(vmem_limit_bytes=8 << 20),
        cost_estimate=pl.CostEstimate(
            flops=4 * rows * width * half, bytes_accessed=12 * rows * width, transcendentals=0
        ),
    )(mine, other, factor, far)


def fetch_kernel(first, queries_ref, out_ref, sem):
    copy = pltpu.make_async_copy(queries_ref.at[pl.ds(first, out_ref.shape[0])], out_ref, sem)
    copy.start()
    copy.wait()


def fetch(queries, first, count):
    return pl.pallas_call(
        functools.partial(fetch_kernel, first),
        out_shape=pltpu.VMEM((count,) + queries.shape[1:], BF16),
        in_specs=[pl.BlockSpec(memory_space=pltpu.HBM)],
        out_specs=pl.BlockSpec(memory_space=pltpu.VMEM),
        scratch_shapes=[pltpu.SemaphoreType.DMA],
        compiler_params=pltpu.CompilerParams(vmem_limit_bytes=2 << 20),
        cost_estimate=pl.CostEstimate(
            flops=0,
            bytes_accessed=2 * count * queries.shape[1] * queries.shape[2],
            transcendentals=0,
        ),
    )(pltpu.with_memory_space_constraint(queries, pltpu.HBM))


def score_kernel(piece, wide, parts, order_ref, *refs):
    grads, refs = refs[:wide], refs[wide:]
    here, (queries_ref, out_ref, held, sums, order, order_sem, sems) = refs[:parts], refs[parts:]
    rows, width = grads[0].shape
    total = queries_ref.shape[0]
    ready = total - held.shape[0]
    late = held.shape[0] // piece

    def copy(i):
        return pltpu.make_async_copy(
            queries_ref.at[pl.ds(ready + i * piece, piece)],
            held.at[pl.ds(i * piece, piece)],
            sems.at[i],
        )

    depth = 2
    for i in range(depth):
        copy(i).start()
    order_copy = pltpu.make_async_copy(order_ref, order, order_sem)
    order_copy.start()
    lanes = wide * GROUP
    weights = jnp.concatenate(
        [
            jnp.concatenate([grad[g : g + GROUP, :] for grad in grads], axis=0)
            for g in range(0, rows, GROUP)
        ],
        axis=1,
    )
    lane = lax.broadcasted_iota(jnp.int32, (GROUP, lanes), 1)
    diagonal = lax.broadcasted_iota(jnp.int32, (GROUP, lanes), 0) == lane % GROUP

    def products(source, first, count):
        block = jnp.concatenate(
            [
                source[pl.ds(first, count), g : g + GROUP, :].reshape(count * GROUP, width)
                for g in range(0, rows, GROUP)
            ],
            axis=1,
        )
        found = lax.dot_general(block, weights, NT, preferred_element_type=F32)
        kept = jnp.where(diagonal, found.reshape(count, GROUP, lanes), 0.0)
        return jnp.sum(kept, axis=1)

    done = 0
    for source in here:
        for first in range(0, source.shape[0], 80):
            sums[done : done + 80, :] = products(source, first, 80)
            done += 80

    def step(i, carry):
        copy(i).wait()

        @pl.when(i + depth < late)
        def _():
            copy(i + depth).start()

        for j in range(0, piece, 80):
            at = pl.multiple_of(i * piece + j, 16)
            sums[pl.ds(ready + at, 80), :] = products(held, at, 80)
        return carry

    lax.fori_loop(0, late, step, 0)

    order_copy.wait()
    row = lax.broadcasted_iota(jnp.int32, (2 * GROUP, lanes), 0)
    source = lax.broadcasted_iota(jnp.int32, (2 * GROUP, lanes), 1) // GROUP
    place = jnp.zeros((2 * GROUP, lanes), F32)
    for k in range(wide):
        goal = order[lax.axis_index("wide") ^ k]
        place += jnp.where((source == k) & (row == goal), 1.0, 0.0)
    place = place.astype(BF16)
    span = out_ref.shape[2]
    blocks = total // span
    for b in range(blocks):
        by_query = sums[b * span : (b + 1) * span, :]
        high = by_query.astype(BF16)
        low = (by_query - high.astype(F32)).astype(BF16)
        scores = lax.dot_general(place, high, NT, preferred_element_type=F32) + lax.dot_general(
            place, low, NT, preferred_element_type=F32
        )
        for m in range(wide):
            out_ref[m * blocks + b] = scores[m : m + 1]


def score_blocks(blocks, piece, order, grads, here, queries):
    wide = len(grads)
    total, rows, width = queries.shape
    late = total - sum(x.shape[0] for x in here)
    vmem = pl.BlockSpec(memory_space=pltpu.VMEM)
    return pl.pallas_call(
        functools.partial(score_kernel, piece, wide, len(here)),
        out_shape=jax.ShapeDtypeStruct((wide * blocks, 1, total // blocks), F32),
        in_specs=[pl.BlockSpec(memory_space=pl.ANY)]
        + [vmem] * (wide + len(here))
        + [pl.BlockSpec(memory_space=pltpu.HBM)],
        out_specs=vmem,
        scratch_shapes=[
            pltpu.VMEM((late, rows, width), BF16),
            pltpu.VMEM((total, wide * GROUP), F32),
            pltpu.SMEM(order.shape, jnp.int32),
            pltpu.SemaphoreType.DMA,
            pltpu.SemaphoreType.DMA((late // piece,)),
        ],
        compiler_params=pltpu.CompilerParams(vmem_limit_bytes=36 << 20),
        cost_estimate=pl.CostEstimate(
            flops=2 * total * rows * width * 128,
            bytes_accessed=2 * total * rows * width,
            transcendentals=0,
        ),
    )(
        order,
        *grads,
        *(pltpu.with_memory_space_constraint(x, pltpu.VMEM) for x in here),
        pltpu.with_memory_space_constraint(queries, pltpu.HBM),
    )


def shared(activations, deltas, act_factor, delta_factor, queries, assignment, padding):
    wide, rep, sub = (lax.axis_size(a) for a in ("wide", "rep", "sub"))
    half = act_factor.shape[1]
    own_block = lax.dynamic_slice_in_dim(act_factor, lax.axis_index("rep") * half, half, axis=0)
    far_block = lax.ppermute(own_block, "rep", [(0, 1), (1, 0)])
    early = queries.shape[0] // 8
    mine, columns, first = row_product(
        padding, deltas[0], activations[0], delta_factor, act_factor, queries, early
    )
    second = fetch(queries, early, early)
    mine, columns, far_block = lax.optimization_barrier((mine, columns, far_block))
    other = lax.ppermute(mine, "sub", [(0, 1), (1, 0)])
    sent = grad_blocks(wide, mine, other, columns, far_block)
    grads = [sent[0]] + [
        lax.ppermute(sent[k], "wide", [(i, i ^ k) for i in range(wide)]) for k in range(1, wide)
    ]
    partial = score_blocks(rep * sub, early, assignment, grads, [first, second], queries)
    gathered = lax.all_to_all(
        partial, ("wide", "rep", "sub"), split_axis=0, concat_axis=0, tiled=True
    )
    return jnp.sum(gathered, axis=0)


def general(activations, deltas, act_factor, delta_factor, queries, assignment, padding):
    seq_dev, tok_dev, _ = activations.shape
    full_length = tok_dev * lax.axis_size("sub")
    token_start = lax.axis_index("sub") * tok_dev
    positions = token_start + lax.broadcasted_iota(jnp.int32, (seq_dev, tok_dev), 1)
    kept_mask = positions < (full_length - padding)[:, None]
    masked = jnp.where(kept_mask[:, :, None], deltas, jnp.zeros((), BF16))
    delta_proj = jnp.einsum(
        "stw,wi->sti", masked, delta_factor, preferred_element_type=F32
    ).astype(BF16)
    act_proj = jnp.einsum(
        "stw,wj->stj",
        activations,
        lax.all_gather(act_factor, "rep", axis=1, tiled=True),
        preferred_element_type=F32,
    ).astype(BF16)
    partial_value = jnp.einsum("sti,stj->sij", delta_proj, act_proj, preferred_element_type=F32)
    summed = lax.psum_scatter(partial_value, "sub", scatter_dimension=2, tiled=True).astype(BF16)
    regrouped = lax.all_to_all(summed, "wide", split_axis=1, concat_axis=0, tiled=True)
    seq_total = regrouped.shape[0]
    grad_rows = regrouped.reshape(seq_total, -1)
    query_rows = queries.reshape(queries.shape[0], -1)
    partial_scores = lax.dot_general(grad_rows, query_rows, NT, preferred_element_type=F32)
    inverse_order = (
        jnp.zeros((seq_total,), jnp.int32)
        .at[assignment]
        .set(jnp.arange(seq_total, dtype=jnp.int32))
    )
    ranked = jnp.take(partial_scores, inverse_order, axis=0)
    by_column = lax.psum_scatter(ranked, ("rep", "sub"), scatter_dimension=1, tiled=True)
    return lax.psum_scatter(by_column, "wide", scatter_dimension=0, tiled=True)


def shards(activations, deltas, act_factor, delta_factor, queries, assignment, padding):
    wide, rep, sub = (lax.axis_size(a) for a in ("wide", "rep", "sub"))
    fits = (
        rep == 2
        and sub == 2
        and wide in (2, 4, 8)
        and activations.shape[:1] == (1,)
        and queries.shape[1] % GROUP == 0
        and queries.shape[0] % (16 * rep * sub) == 0
        and act_factor.shape[1] % 128 == 0
    )
    body = shared if fits else general
    return body(activations, deltas, act_factor, delta_factor, queries, assignment, padding)


def solution(mesh):
    placed = (
        P(("parts", "wide"), "sub", None),
        P(("parts", "wide"), "sub", None),
        P(None, "rep"),
        P(None, "rep"),
        P(None, ("rep", "wide"), "sub"),
        P("parts"),
        P(("parts", "wide")),
    )
    return jax.shard_map(
        shards,
        mesh=mesh,
        in_specs=placed,
        out_specs=P(("parts", "wide"), ("rep", "sub")),
        check_vma=False,
    )
```

time: 138 us -> 45.4 us (0.33)
  local copies, waits for them, and re-layouts: 45.6 us -> 1.48 us
  waiting for transfers between devices: 27 us -> 4.88 us
  Pallas kernels: 0 us -> 21.4 us
  matrix products: 21 us -> 0 us
  between operations: 14.3 us -> 0.72 us
  blocking collectives: 22 us -> 9.14 us
  starting transfers between devices: 5.09 us -> 7.53 us
  other arithmetic: 2.47 us -> 0.04 us
    unnamed x16 -> x2, local copies, waits for them, and re-layouts: 43.4 us -> 0.01 us
    pallas_call x0 -> x4, Pallas kernels: none -> 21.4 us  [the longest x1 15 us: score_blocks(): pl.pallas_call(functools.partial(score_kernel, piece, wide, len(here)), o...]
    unnamed x3 -> x0, waiting for transfers between devices: 21.1 us -> none
    dot_general x3 -> x0, matrix products: 21 us -> none  [the longest x1 17.5 us: shards(): lax.dot_general(grad_rows, query_rows, (((1,), (1,)), ((), ())), preferre...]
    unnamed x1 -> x0, blocking collectives: 11.8 us -> none
    all_gather x1 -> x0, blocking collectives: 10.2 us -> none  [shards(): lax.all_gather(act_factor, 'rep', axis=1, tiled=True)]
    all_to_all x0 -> x1, blocking collectives: none -> 9.14 us  [shared(): lax.all_to_all(partial, ('wide', 'rep', 'sub'), split_axis=0, concat_axis...]
    ppermute x0 -> x5, starting transfers between devices: none -> 7.53 us  [the longest x3 4.45 us: shared(): lax.ppermute(sent[k], 'wide', [(i, i ^ k) for i in range(wide)])]
  transfers between devices with their start and end apart: 3 -> 5, of which waited for: 2 -> 3; matrix products, arithmetic and copies ran while one was open for 29% -> 0% of each run, Pallas kernels for 0% -> 13%
where the time goes in v2:
time: 45.4 us; the launch traced here: 45.1 us
  Pallas kernels  21.4 us (47%)
  blocking collectives  9.14 us (20%)
  starting transfers between devices  7.53 us (17%)
  waiting for transfers between devices  4.88 us (11%)
  local copies, waits for them, and re-layouts  1.48 us (3%)
  between operations  0.72 us (2%)
    pallas_call x1, Pallas kernels, score_blocks(): pl.pallas_call(functools.partial(score_kernel, piece, wide, len(here)), o...  15 us
    all_to_all x1, blocking collectives, shared(): lax.all_to_all(partial, ('wide', 'rep', 'sub'), split_axis=0, concat_axis...  9.14 us
    ppermute x3, starting transfers between devices, shared(): lax.ppermute(sent[k], 'wide', [(i, i ^ k) for i in range(wide)])  4.45 us
    pallas_call x1, Pallas kernels, row_product(): pl.pallas_call(row_product_kernel, out_shape=(jax.ShapeDtypeStruct((rows,...  3.45 us
    ppermute x1, starting transfers between devices, shared(): far_block = lax.ppermute(own_block, 'rep', [(0, 1), (1, 0)])  3 us
    ppermute x3, waiting for transfers between devices, shared(): lax.ppermute(sent[k], 'wide', [(i, i ^ k) for i in range(wide)])  2.98 us
    pallas_call x1, Pallas kernels, fetch(): pl.pallas_call(functools.partial(fetch_kernel, first), out_shape=pltpu.VM...  2.49 us
    ppermute x1, waiting for transfers between devices, shared(): other = lax.ppermute(mine, 'sub', [(0, 1), (1, 0)])  1.9 us
  transfers between devices with their start and end apart: 5, of which 3 were waited for; matrix products, arithmetic and copies ran while one was open for 0% of the time, Pallas kernels for 13%

profile of v2, /device:TPU:0, one launch (start us, length us, event | category | flops | bytes accessed | tf_op | source)
XLA Modules:
  0.0 45.1 jit_solution(3722756469299227779)
XLA Ops:
  0.0 0.9 %constant_dynamic-slice_fusion = bf16[256,256]{1,0:T(8,128)(2,1)S(1)} fusion(bf16[512,256]{1,0:T(8,128)(2,1)} %col_factor_ref.1, s32[]{:T(128)S(6)} %select_n.3), kind=kLoop, calls=%fused_computation | loop fusion | bytes 262148 | tf_op jit(solution)/shard_map/dynamic_slice | solution.py:289
  0.9 3.0 %collective-permute-start = (bf16[256,256]{1,0:T(8,128)(2,1)S(1)}, bf16[256,256]{1,0:T(8,128)(2,1)S(1)}, u32[]{:S(2)}, u32[]{:S(2)}) collective-permute-start(bf16[256,256]{1,0:T(8,128)(2,1)S(1)} %constant_dynamic-slice_fusion), channel_id=1, source_target_pairs={{0,2},{2,0},{1,3},{3,1},{4,6},{6,4},{5,7},{7,5},{8,10},{10,8},{9,1... | collective-permute-start | bytes 393224 | tf_op jit(solution)/shard_map/ppermute | solution.py:290
  4.6 3.4 %shard_map.73 = (f32[256,512]{1,0:T(8,128)S(1)}, bf16[512,256]{1,0:T(8,128)(2,1)S(1)}, bf16[160,64,256]{2,1,0:T(8,128)(2,1)S(1)}) custom-call(s32[1]{0:T(128)S(6)} %copy.8.pad_ref, bf16[1024,512]{1,0:T(8,128)(2,1)} %bitcast.2, bf16[1024,512]{1,0:T(8,128)(2,1)} %bitcast.3, bf16[512,256]{1,0:T(8,128)(2,1)} %row_factor_ref.1, bf16[512,256]{1,0:T(8,128)(2,1)} %col_factor_ref.1, ...), custom_call_target="tpu_custom_call" | custom-call | flops 536870912 | bytes 2097152 | tf_op jit(solution)/shard_map/pallas_call | solution.py:72
  8.0 0.0 collective-permute-done.far_ref
  8.0 0.1 collective-permute-start.1
  8.1 1.9 %collective-permute-done.1.other_ref = f32[256,512]{1,0:T(8,128)S(1)} collective-permute-done((f32[256,512]{1,0:T(8,128)S(1)}, f32[256,512]{1,0:T(8,128)S(1)}, u32[]{:S(2)}, u32[]{:S(2)}) %collective-permute-start.1) | collective-permute-done | bytes 524320 | tf_op jit(solution)/shard_map/ppermute | solution.py:297
  10.0 0.5 shard_map.74
  10.5 1.6 %collective-permute-start.2 = (bf16[64,256]{1,0:T(8,128)(2,1)S(1)}, bf16[64,256]{1,0:T(8,128)(2,1)S(1)}, u32[]{:S(2)}, u32[]{:S(2)}) collective-permute-start(bf16[64,256]{1,0:T(8,128)(2,1)S(1)} %get-tuple-element.21), channel_id=1, source_target_pairs={{0,4},{4,0},{8,12},{12,8},{1,5},{5,1},{9,13},{13,9},{2,6},{6,2},{1... | collective-permute-start | bytes 98312 | tf_op jit(solution)/shard_map/ppermute | solution.py:300
  12.1 2.6 %collective-permute-start.3 = (bf16[64,256]{1,0:T(8,128)(2,1)S(1)}, bf16[64,256]{1,0:T(8,128)(2,1)S(1)}, u32[]{:S(2)}, u32[]{:S(2)}) collective-permute-start(bf16[64,256]{1,0:T(8,128)(2,1)S(1)} %get-tuple-element.22), channel_id=1, source_target_pairs={{0,8},{4,12},{8,0},{12,4},{1,9},{5,13},{9,1},{13,5},{2,10},{6,14},... | collective-permute-start | bytes 98312 | tf_op jit(solution)/shard_map/ppermute | solution.py:300
  14.7 0.0 copy-start
  14.7 0.2 collective-permute-start.4
  14.9 2.5 %shard_map.75.refs_5_ = bf16[160,64,256]{2,1,0:T(8,128)(2,1)S(1)} custom-call(bf16[1280,64,256]{2,1,0:T(8,128)(2,1)} %refs_6_.1), custom_call_target="tpu_custom_call" | custom-call | bytes 5242880 | tf_op jit(solution)/shard_map/pallas_call | solution.py:154
  17.4 0.0 collective-permute-done.2.refs_1_
  17.4 0.1 collective-permute-done.3.refs_2_
  17.5 2.9 %collective-permute-done.4.refs_3_ = bf16[64,256]{1,0:T(8,128)(2,1)S(1)} collective-permute-done((bf16[64,256]{1,0:T(8,128)(2,1)S(1)}, bf16[64,256]{1,0:T(8,128)(2,1)S(1)}, u32[]{:S(2)}, u32[]{:S(2)}) %collective-permute-start.4) | collective-permute-done | bytes 32800 | tf_op jit(solution)/shard_map/ppermute | solution.py:300
  20.4 0.0 copy-done
  20.4 15.0 %shard_map.76 = f32[16,1,320]{2,1,0:T(1,128)S(1)} custom-call(s32[4]{0:T(128)S(1)} %copy-done, bf16[64,256]{1,0:T(8,128)(2,1)S(1)} %get-tuple-element.20.refs_0_, bf16[64,256]{1,0:T(8,128)(2,1)S(1)} %collective-permute-done.2.refs_1_, bf16[64,256]{1,0:T(8,128)(2,1)S(1)} %collective-permute-done.3.refs_2_, ...), custom_call_target="tpu_custom_call" | custom-call | flops 5368709120 | bytes 41943040 | tf_op jit(solution)/shard_map/pallas_call | solution.py:258
  35.4 9.1 %all_to_all.5 = f32[16,1,320]{2,1,0:T(1,128)S(1)} all-to-all(f32[16,1,320]{2,1,0:T(1,128)S(1)} %shard_map.76), channel_id=1, replica_groups=mesh['parts'=2,'wide'=4,'rep'=2,'sub'=2] {'wide','rep','sub'}, dimensions={0} | all-to-all | bytes 40960 | tf_op jit(solution)/shard_map/all_to_all | solution.py:303
  44.6 0.6 %reduce_sum.12 = f32[1,320]{1,0:T(1,128)} reshape(f32[320]{0:T(512)S(1)} %reduce_sum.11) | data formatting | bytes 2560 | tf_op jit(solution)/shard_map/reduce_sum | solution.py:306
  (1 shorter events, 0.0 us)
Async XLA Ops:
  0.9 7.1 %collective-permute-start = (bf16[256,256]{1,0:T(8,128)(2,1)S(1)}, bf16[256,256]{1,0:T(8,128)(2,1)S(1)}, u32[]{:S(2)}, u32[]{:S(2)}) collective-permute-start(bf16[256,256]{1,0:T(8,128)(2,1)S(1)} %constant_dynamic-slice_fusion), channel_id=1, source_target_pairs={{0,2},{2,0},{1,3},{3,1},{4,6},{6,4},{5,7},{7,5},{8,10},{10,8},{9,1... | collective-permute-start | bytes 393224 | tf_op jit(solution)/shard_map/ppermute | solution.py:290
  8.0 2.0 %collective-permute-start.1 = (f32[256,512]{1,0:T(8,128)S(1)}, f32[256,512]{1,0:T(8,128)S(1)}, u32[]{:S(2)}, u32[]{:S(2)}) collective-permute-start(f32[256,512]{1,0:T(8,128)S(1)} %get-tuple-element.17.mine_ref), channel_id=1, source_target_pairs={{0,1},{1,0},{2,3},{3,2},{4,5},{5,4},{6,7},{7,6},{8,9},{9,8},{10,11... | collective-permute-start | bytes 1572872 | tf_op jit(solution)/shard_map/ppermute | solution.py:297
  10.5 7.0 %collective-permute-start.2 = (bf16[64,256]{1,0:T(8,128)(2,1)S(1)}, bf16[64,256]{1,0:T(8,128)(2,1)S(1)}, u32[]{:S(2)}, u32[]{:S(2)}) collective-permute-start(bf16[64,256]{1,0:T(8,128)(2,1)S(1)} %get-tuple-element.21), channel_id=1, source_target_pairs={{0,4},{4,0},{8,12},{12,8},{1,5},{5,1},{9,13},{13,9},{2,6},{6,2},{1... | collective-permute-start | bytes 98312 | tf_op jit(solution)/shard_map/ppermute | solution.py:300
  12.1 5.4 %collective-permute-start.3 = (bf16[64,256]{1,0:T(8,128)(2,1)S(1)}, bf16[64,256]{1,0:T(8,128)(2,1)S(1)}, u32[]{:S(2)}, u32[]{:S(2)}) collective-permute-start(bf16[64,256]{1,0:T(8,128)(2,1)S(1)} %get-tuple-element.22), channel_id=1, source_target_pairs={{0,8},{4,12},{8,0},{12,4},{1,9},{5,13},{9,1},{13,5},{2,10},{6,14},... | collective-permute-start | bytes 98312 | tf_op jit(solution)/shard_map/ppermute | solution.py:300
  14.7 5.7 %copy-start = (s32[4]{0:T(128)S(1)}, s32[4]{0:T(128)}, u32[]{:S(2)}) copy-start(s32[4]{0:T(128)} %order_ref.1) | copy-start | bytes 52
  14.7 5.7 %collective-permute-start.4 = (bf16[64,256]{1,0:T(8,128)(2,1)S(1)}, bf16[64,256]{1,0:T(8,128)(2,1)S(1)}, u32[]{:S(2)}, u32[]{:S(2)}) collective-permute-start(bf16[64,256]{1,0:T(8,128)(2,1)S(1)} %get-tuple-element.23), channel_id=1, source_target_pairs={{0,12},{4,8},{8,4},{12,0},{1,13},{5,9},{9,5},{13,1},{2,14},{6,10},... | collective-permute-start | bytes 98312 | tf_op jit(solution)/shard_map/ppermute | solution.py:300

commit v3 on v2

--- a/solution.py
+++ b/solution.py
@@ -166,27 +166,101 @@
     )(pltpu.with_memory_space_constraint(queries, pltpu.HBM))
 
 
-def score_kernel(piece, wide, parts, order_ref, *refs):
+def exchange_kernel(wide, order_ref, *refs):
+    grads, (out_ref, order, sem) = refs[:wide], refs[wide:]
+    rows, width = grads[0].shape
+    part, parts = lax.axis_index("parts"), lax.axis_size("parts")
+    share = rows // parts
+    copy = pltpu.make_async_copy(order_ref, order, sem)
+    copy.start()
+    first = pl.multiple_of((1 - part) * share, share)
+    for k in range(wide):
+        out_ref[k * share : (k + 1) * share, :] = grads[k][pl.ds(first, share), :]
+    copy.wait()
+    row = lax.broadcasted_iota(jnp.int32, (GROUP, width), 0)
+    lane = lax.broadcasted_iota(jnp.int32, (GROUP, width), 1)
+    tags = jnp.zeros((GROUP, width), F32)
+    for k in range(wide):
+        goal = part * wide + order[lax.axis_index("wide") ^ k]
+        tags += jnp.where((row == k) & (lane == goal), 1.0, 0.0)
+    out_ref[wide * share :, :] = tags.astype(BF16)
+
+
+def exchange_block(parts, order, grads):
+    wide = len(grads)
+    rows, width = grads[0].shape
+    vmem = pl.BlockSpec(memory_space=pltpu.VMEM)
+    return pl.pallas_call(
+        functools.partial(exchange_kernel, wide),
+        out_shape=jax.ShapeDtypeStruct((wide * rows // parts + GROUP, width), BF16),
+        in_specs=[pl.BlockSpec(memory_space=pl.ANY)] + [vmem] * wide,
+        out_specs=vmem,
+        scratch_shapes=[pltpu.SMEM(order.shape, jnp.int32), pltpu.SemaphoreType.DMA],
+        compiler_params=pltpu.CompilerParams(vmem_limit_bytes=2 << 20),
+        cost_estimate=pl.CostEstimate(
+            flops=0, bytes_accessed=4 * wide * rows * width, transcendentals=0
+        ),
+    )(order, *grads)
+
+
+def joined_rows(source, first, count, start, rows):
+    width = source.shape[2]
+    return jnp.concatenate(
+        [
+            source[pl.ds(first, count), pl.ds(start + g, GROUP), :].reshape(count * GROUP, width)
+            for g in range(0, rows, GROUP)
+        ],
+        axis=1,
+    )
+
+
+def group_sums(lines, weights, count):
+    lanes = weights.shape[0]
+    lane = lax.broadcasted_iota(jnp.int32, (GROUP, lanes), 1)
+    diagonal = lax.broadcasted_iota(jnp.int32, (GROUP, lanes), 0) == lane % GROUP
+    found = lax.dot_general(lines, weights, NT, preferred_element_type=F32)
+    return jnp.sum(jnp.where(diagonal, found.reshape(count, GROUP, lanes), 0.0), axis=1)
+
+
+def add_up(place, sums):
+    high = sums.astype(BF16)
+    low = (sums - high.astype(F32)).astype(BF16)
+    return lax.dot_general(place, high, NT, preferred_element_type=F32) + lax.dot_general(
+        place, low, NT, preferred_element_type=F32
+    )
+
+
+def place_of(block_ref, lanes, first):
+    tags = block_ref[block_ref.shape[0] - GROUP :, :]
+    source = lax.broadcasted_iota(jnp.int32, (GROUP, lanes), 1) // GROUP - first
+    owner = source == lax.broadcasted_iota(jnp.int32, (GROUP, lanes), 0)
+    return lax.dot_general(
+        tags, owner.astype(F32).astype(BF16), TN, preferred_element_type=F32
+    )[:GROUP]
+
+
+LOOPS = 2
+
+
+def local_score_kernel(wide, sets, tags_ref, *refs):
     grads, refs = refs[:wide], refs[wide:]
-    here, (queries_ref, out_ref, held, sums, order, order_sem, sems) = refs[:parts], refs[parts:]
+    here, (queries_ref, out_ref, held_ref, sums, sems) = refs[:sets], refs[sets:]
     rows, width = grads[0].shape
-    total = queries_ref.shape[0]
-    ready = total - held.shape[0]
-    late = held.shape[0] // piece
+    part, parts = lax.axis_index("parts"), lax.axis_size("parts")
+    share = rows // parts
+    done = sum(source.shape[0] for source in here)
+    half = held_ref.shape[0] // 2
+    own = pl.multiple_of(part * share, share)
 
     def copy(i):
         return pltpu.make_async_copy(
-            queries_ref.at[pl.ds(ready + i * piece, piece)],
-            held.at[pl.ds(i * piece, piece)],
+            queries_ref.at[pl.ds(done + i * half, half), pl.ds(own, share), :],
+            held_ref.at[pl.ds(i * half, half)],
             sems.at[i],
         )
 
-    depth = 2
-    for i in range(depth):
+    for i in range(2):
         copy(i).start()
-    order_copy = pltpu.make_async_copy(order_ref, order, order_sem)
-    order_copy.start()
-    lanes = wide * GROUP
     weights = jnp.concatenate(
         [
             jnp.concatenate([grad[g : g + GROUP, :] for grad in grads], axis=0)
@@ -194,114 +268,193 @@
         ],
         axis=1,
     )
-    lane = lax.broadcasted_iota(jnp.int32, (GROUP, lanes), 1)
-    diagonal = lax.broadcasted_iota(jnp.int32, (GROUP, lanes), 0) == lane % GROUP
-
-    def products(source, first, count):
-        block = jnp.concatenate(
-            [
-                source[pl.ds(first, count), g : g + GROUP, :].reshape(count * GROUP, width)
-                for g in range(0, rows, GROUP)
-            ],
-            axis=1,
+    def step(i, carry):
+        counts = [source.shape[0] // LOOPS for source in here]
+        lines = [
+            joined_rows(source, pl.multiple_of(i * count, 8), count, 0, rows)
+            for source, count in zip(here, counts)
+        ]
+        found = group_sums(jnp.concatenate(lines, axis=0), weights, sum(counts))
+        at, taken = 0, 0
+        for count in counts:
+            to = pl.multiple_of(at + i * count, 8)
+            sums[pl.ds(to, count), :] = found[taken : taken + count]
+            at, taken = at + count * LOOPS, taken + count
+        return carry
+
+    lax.fori_loop(0, LOOPS, step, 0)
+    out_ref[...] = add_up(place_of(tags_ref, wide * GROUP, 0).astype(BF16), sums[...])
+
+    def finish(i, carry):
+        copy(i).wait()
+        return carry
+
+    lax.fori_loop(0, 2, finish, 0)
+
+
+def local_scores(parts, tagged, grads, here, queries, count):
+    wide = len(grads)
+    rows, width = grads[0].shape
+    done = sum(x.shape[0] for x in here)
+    vmem = pl.BlockSpec(memory_space=pltpu.VMEM)
+    return pl.pallas_call(
+        functools.partial(local_score_kernel, wide, len(here)),
+        out_shape=(
+            jax.ShapeDtypeStruct((GROUP, done), F32),
+            pltpu.VMEM((count, rows // parts, width), BF16),
+        ),
+        in_specs=[vmem] * (1 + wide + len(here))
+        + [pl.BlockSpec(memory_space=pltpu.HBM)],
+        out_specs=(vmem, vmem),
+        scratch_shapes=[
+            pltpu.VMEM((done, wide * GROUP), F32),
+            pltpu.SemaphoreType.DMA((2,)),
+        ],
+        compiler_params=pltpu.CompilerParams(vmem_limit_bytes=10 << 20),
+        cost_estimate=pl.CostEstimate(
+            flops=2 * done * rows * width * 128,
+            bytes_accessed=2 * (done + count) * rows * width,
+            transcendentals=0,
+        ),
+    )(
+        tagged,
+        *grads,
+        *(pltpu.with_memory_space_constraint(x, pltpu.VMEM) for x in here),
+        pltpu.with_memory_space_constraint(queries, pltpu.HBM),
+    )
+
+
+def shared_score_kernel(wide, pieces, tags_ref, *refs):
+    grads, refs = refs[:wide], refs[wide:]
+    far_ref, local_ref, here_ref, queries_ref, out_ref, held, sums, sems = refs
+    rows, width = grads[0].shape
+    part, parts = lax.axis_index("parts"), lax.axis_size("parts")
+    share = rows // parts
+    local = local_ref.shape[1]
+    ready = here_ref.shape[0]
+    piece = held.shape[0] // pieces
+    own = pl.multiple_of(part * share, share)
+
+    def copy(i):
+        return pltpu.make_async_copy(
+            queries_ref.at[pl.ds(local + ready + i * piece, piece), pl.ds(own, share), :],
+            held.at[pl.ds(i * piece, piece)],
+            sems.at[i],
         )
-        found = lax.dot_general(block, weights, NT, preferred_element_type=F32)
-        kept = jnp.where(diagonal, found.reshape(count, GROUP, lanes), 0.0)
-        return jnp.sum(kept, axis=1)
-
-    done = 0
-    for source in here:
-        for first in range(0, source.shape[0], 80):
-            sums[done : done + 80, :] = products(source, first, 80)
-            done += 80
-
-    def step(i, carry):
+
+    depth = min(2, pieces)
+    for i in range(depth):
+        copy(i).start()
+    lanes = parts * wide * GROUP
+    weights = jnp.concatenate(
+        [
+            jnp.concatenate(
+                [grad[pl.ds(own + g, GROUP), :] for grad in grads]
+                + [far_ref[k * share + g : k * share + g + GROUP, :] for k in range(wide)],
+                axis=0,
+            )
+            for g in range(0, share, GROUP)
+        ],
+        axis=1,
+    )
+
+    def ready_step(i, carry):
+        at = pl.multiple_of(i * piece, GROUP)
+        lines = joined_rows(here_ref, at, piece, 0, share)
+        sums[pl.ds(local + at, piece), :] = group_sums(lines, weights, piece)
+        return carry
+
+    lax.fori_loop(0, ready // piece, ready_step, 0)
+
+    def late_step(i, carry):
         copy(i).wait()
 
-        @pl.when(i + depth < late)
+        @pl.when(i + depth < pieces)
         def _():
             copy(i + depth).start()
 
-        for j in range(0, piece, 80):
-            at = pl.multiple_of(i * piece + j, 16)
-            sums[pl.ds(ready + at, 80), :] = products(held, at, 80)
+        at = pl.multiple_of(i * piece, GROUP)
+        lines = joined_rows(held, at, piece, 0, share)
+        sums[pl.ds(local + ready + at, piece), :] = group_sums(lines, weights, piece)
         return carry
 
-    lax.fori_loop(0, late, step, 0)
-
-    order_copy.wait()
-    row = lax.broadcasted_iota(jnp.int32, (2 * GROUP, lanes), 0)
-    source = lax.broadcasted_iota(jnp.int32, (2 * GROUP, lanes), 1) // GROUP
-    place = jnp.zeros((2 * GROUP, lanes), F32)
-    for k in range(wide):
-        goal = order[lax.axis_index("wide") ^ k]
-        place += jnp.where((source == k) & (row == goal), 1.0, 0.0)
-    place = place.astype(BF16)
+    lax.fori_loop(0, pieces, late_step, 0)
+
+    place = (place_of(tags_ref, lanes, 0) + place_of(far_ref, lanes, wide)).astype(BF16)
     span = out_ref.shape[2]
-    blocks = total // span
+    blocks = queries_ref.shape[0] // span
     for b in range(blocks):
-        by_query = sums[b * span : (b + 1) * span, :]
-        high = by_query.astype(BF16)
-        low = (by_query - high.astype(F32)).astype(BF16)
-        scores = lax.dot_general(place, high, NT, preferred_element_type=F32) + lax.dot_general(
-            place, low, NT, preferred_element_type=F32
-        )
-        for m in range(wide):
-            out_ref[m * blocks + b] = scores[m : m + 1]
-
-
-def score_blocks(blocks, piece, order, grads, here, queries):
+        if (b + 1) * span <= local:
+            for m in range(parts * wide):
+                out_ref[m * blocks + b] = local_ref[m : m + 1, b * span : (b + 1) * span]
+        else:
+            scores = add_up(place, sums[b * span : (b + 1) * span, :])
+            for m in range(parts * wide):
+                out_ref[m * blocks + b] = scores[m : m + 1]
+
+
+def shared_scores(parts, blocks, pieces, tagged, grads, far, local, here, queries):
     wide = len(grads)
-    total, rows, width = queries.shape
-    late = total - sum(x.shape[0] for x in here)
+    rows, width = grads[0].shape
+    total = queries.shape[0]
+    late = total - local.shape[1] - here.shape[0]
     vmem = pl.BlockSpec(memory_space=pltpu.VMEM)
     return pl.pallas_call(
-        functools.partial(score_kernel, piece, wide, len(here)),
-        out_shape=jax.ShapeDtypeStruct((wide * blocks, 1, total // blocks), F32),
-        in_specs=[pl.BlockSpec(memory_space=pl.ANY)]
-        + [vmem] * (wide + len(here))
+        functools.partial(shared_score_kernel, wide, pieces),
+        out_shape=jax.ShapeDtypeStruct((parts * wide * blocks, 1, total // blocks), F32),
+        in_specs=[vmem] * (wide + 4)
         + [pl.BlockSpec(memory_space=pltpu.HBM)],
         out_specs=vmem,
         scratch_shapes=[
-            pltpu.VMEM((late, rows, width), BF16),
-            pltpu.VMEM((total, wide * GROUP), F32),
-            pltpu.SMEM(order.shape, jnp.int32),
-            pltpu.SemaphoreType.DMA,
-            pltpu.SemaphoreType.DMA((late // piece,)),
+            pltpu.VMEM((late, rows // parts, width), BF16),
+            pltpu.VMEM((total, parts * wide * GROUP), F32),
+            pltpu.SemaphoreType.DMA((pieces,)),
         ],
-        compiler_params=pltpu.CompilerParams(vmem_limit_bytes=36 << 20),
+        compiler_params=pltpu.CompilerParams(vmem_limit_bytes=20 << 20),
         cost_estimate=pl.CostEstimate(
             flops=2 * total * rows * width * 128,
-            bytes_accessed=2 * total * rows * width,
+            bytes_accessed=2 * late * rows * width,
             transcendentals=0,
         ),
     )(
-        order,
+        tagged,
         *grads,
-        *(pltpu.with_memory_space_constraint(x, pltpu.VMEM) for x in here),
+        far,
+        local,
+        pltpu.with_memory_space_constraint(here, pltpu.VMEM),
         pltpu.with_memory_space_constraint(queries, pltpu.HBM),
     )
 
 
 def shared(activations, deltas, act_factor, delta_factor, queries, assignment, padding):
-    wide, rep, sub = (lax.axis_size(a) for a in ("wide", "rep", "sub"))
+    parts, wide, rep, sub = (lax.axis_size(a) for a in ("parts", "wide", "rep", "sub"))
     half = act_factor.shape[1]
+    early = queries.shape[0] // 8
+    later = 3 * early
     own_block = lax.dynamic_slice_in_dim(act_factor, lax.axis_index("rep") * half, half, axis=0)
     far_block = lax.ppermute(own_block, "rep", [(0, 1), (1, 0)])
-    early = queries.shape[0] // 8
     mine, columns, first = row_product(
         padding, deltas[0], activations[0], delta_factor, act_factor, queries, early
     )
-    second = fetch(queries, early, early)
+    second = fetch(queries, early, early // 2)
+    third = fetch(queries, 3 * early // 2, early // 2)
     mine, columns, far_block = lax.optimization_barrier((mine, columns, far_block))
     other = lax.ppermute(mine, "sub", [(0, 1), (1, 0)])
+    other, second = lax.optimization_barrier((other, second))
     sent = grad_blocks(wide, mine, other, columns, far_block)
     grads = [sent[0]] + [
         lax.ppermute(sent[k], "wide", [(i, i ^ k) for i in range(wide)]) for k in range(1, wide)
     ]
-    partial = score_blocks(rep * sub, early, assignment, grads, [first, second], queries)
+    tagged = exchange_block(parts, assignment, grads)
+    far = lax.ppermute(tagged, "parts", [(0, 1), (1, 0)])
+    local, held = local_scores(
+        parts, tagged, grads, [first, second, third], queries, later
+    )
+    partial = shared_scores(
+        parts, rep * sub, 3, tagged, grads, far, local, held, queries
+    )
     gathered = lax.all_to_all(
-        partial, ("wide", "rep", "sub"), split_axis=0, concat_axis=0, tiled=True
+        partial, ("parts", "wide", "rep", "sub"), split_axis=0, concat_axis=0, tiled=True
     )
     return jnp.sum(gathered, axis=0)
 
@@ -340,14 +493,15 @@
 
 
 def shards(activations, deltas, act_factor, delta_factor, queries, assignment, padding):
-    wide, rep, sub = (lax.axis_size(a) for a in ("wide", "rep", "sub"))
+    parts, wide, rep, sub = (lax.axis_size(a) for a in ("parts", "wide", "rep", "sub"))
     fits = (
-        rep == 2
+        parts == 2
+        and rep == 2
         and sub == 2
-        and wide in (2, 4, 8)
-        and activations.shape[:1] == (1,)
-        and queries.shape[1] % GROUP == 0
-        and queries.shape[0] % (16 * rep * sub) == 0
+        and wide in (2, 4)
+        and activations.shape[0] == 1
+        and queries.shape[1] % (parts * GROUP) == 0
+        and queries.shape[0] % (16 * GROUP) == 0
         and act_factor.shape[1] % 128 == 0
     )
     body = shared if fits else general

time: 45.4 us -> 41.7 us (0.919)
  Pallas kernels: 21.4 us -> 17.1 us
  starting transfers between devices: 7.53 us -> 9.14 us
  waiting for transfers between devices: 4.88 us -> 3.87 us
    pallas_call x1 -> x3, Pallas kernels: 15 us -> 9.72 us  [the longest x1 5.67 us: shared_scores(): pl.pallas_call(functools.partial(shared_score_kernel, wide, pieces), out_...]
    ppermute x1, waiting for transfers between devices: 1.9 us -> 0.14 us  [shared(): other = lax.ppermute(mine, 'sub', [(0, 1), (1, 0)])]
    ppermute x0 -> x1, starting transfers between devices: none -> 1.59 us  [shared(): far = lax.ppermute(tagged, 'parts', [(0, 1), (1, 0)])]
    pallas_call x1 -> x2, Pallas kernels: 2.49 us -> 3.5 us  [fetch(): pl.pallas_call(functools.partial(fetch_kernel, first), out_shape=pltpu.VM...]
    ppermute x3, waiting for transfers between devices: 2.98 us -> 3.73 us  [shared(): lax.ppermute(sent[k], 'wide', [(i, i ^ k) for i in range(wide)])]
  transfers between devices with their start and end apart: 5 -> 6, of which waited for: 3 -> 3; matrix products, arithmetic and copies ran while one was open for 0% -> 0% of each run, Pallas kernels for 13% -> 25%
where the time goes in v3:
time: 41.7 us; the launch traced here: 41.4 us
  Pallas kernels  17.1 us (41%)
  starting transfers between devices  9.14 us (22%)
  blocking collectives  9.03 us (22%)
  waiting for transfers between devices  3.87 us (9%)
  local copies, waits for them, and re-layouts  1.48 us (4%)
  between operations  0.75 us (2%)
    all_to_all x1, blocking collectives, shared(): lax.all_to_all(partial, ('parts', 'wide', 'rep', 'sub'), split_axis=0, co...  9.03 us
    pallas_call x1, Pallas kernels, shared_scores(): pl.pallas_call(functools.partial(shared_score_kernel, wide, pieces), out_...  5.67 us
    ppermute x3, starting transfers between devices, shared(): lax.ppermute(sent[k], 'wide', [(i, i ^ k) for i in range(wide)])  4.48 us
    ppermute x3, waiting for transfers between devices, shared(): lax.ppermute(sent[k], 'wide', [(i, i ^ k) for i in range(wide)])  3.73 us
    pallas_call x2, Pallas kernels, fetch(): pl.pallas_call(functools.partial(fetch_kernel, first), out_shape=pltpu.VM...  3.5 us
    pallas_call x1, Pallas kernels, local_scores(): pl.pallas_call(functools.partial(local_score_kernel, wide, len(here)), ou...  3.48 us
    pallas_call x1, Pallas kernels, row_product(): pl.pallas_call(row_product_kernel, out_shape=(jax.ShapeDtypeStruct((rows,...  3.45 us
    ppermute x1, starting transfers between devices, shared(): far_block = lax.ppermute(own_block, 'rep', [(0, 1), (1, 0)])  3 us
  transfers between devices with their start and end apart: 6, of which 3 were waited for; matrix products, arithmetic and copies ran while one was open for 0% of the time, Pallas kernels for 25%

profile of v3, /device:TPU:0, one launch (start us, length us, event | category | flops | bytes accessed | tf_op | source)
XLA Modules:
  0.0 41.4 jit_solution(9496089409888550449)
XLA Ops:
  0.0 0.9 %constant_dynamic-slice_fusion = bf16[256,256]{1,0:T(8,128)(2,1)S(1)} fusion(bf16[512,256]{1,0:T(8,128)(2,1)} %col_factor_ref.1, s32[]{:T(128)S(6)} %select_n.3), kind=kLoop, calls=%fused_computation | loop fusion | bytes 262148 | tf_op jit(solution)/shard_map/dynamic_slice | solution.py:434
  0.9 3.0 %collective-permute-start = (bf16[256,256]{1,0:T(8,128)(2,1)S(1)}, bf16[256,256]{1,0:T(8,128)(2,1)S(1)}, u32[]{:S(2)}, u32[]{:S(2)}) collective-permute-start(bf16[256,256]{1,0:T(8,128)(2,1)S(1)} %constant_dynamic-slice_fusion), channel_id=1, source_target_pairs={{0,2},{2,0},{1,3},{3,1},{4,6},{6,4},{5,7},{7,5},{8,10},{10,8},{9,1... | collective-permute-start | bytes 393224 | tf_op jit(solution)/shard_map/ppermute | solution.py:435
  4.6 3.4 %shard_map.73 = (f32[256,512]{1,0:T(8,128)S(1)}, bf16[512,256]{1,0:T(8,128)(2,1)S(1)}, bf16[160,64,256]{2,1,0:T(8,128)(2,1)S(1)}) custom-call(s32[1]{0:T(128)S(6)} %copy.8.pad_ref, bf16[1024,512]{1,0:T(8,128)(2,1)} %bitcast.2, bf16[1024,512]{1,0:T(8,128)(2,1)} %bitcast.3, bf16[512,256]{1,0:T(8,128)(2,1)} %row_factor_ref.1, bf16[512,256]{1,0:T(8,128)(2,1)} %col_factor_ref.1, ...), custom_call_target="tpu_custom_call" | custom-call | flops 536870912 | bytes 2097152 | tf_op jit(solution)/shard_map/pallas_call | solution.py:72
  8.0 0.0 collective-permute-done.far_ref
  8.0 0.1 collective-permute-start.1
  8.1 1.8 %shard_map.74.refs_5_ = bf16[80,64,256]{2,1,0:T(8,128)(2,1)S(1)} custom-call(bf16[1280,64,256]{2,1,0:T(8,128)(2,1)} %refs_7_.3), custom_call_target="tpu_custom_call" | custom-call | bytes 2621440 | tf_op jit(solution)/shard_map/pallas_call | solution.py:154
  9.9 0.1 collective-permute-done.1.other_ref
  10.0 0.5 %shard_map.75 = (bf16[64,256]{1,0:T(8,128)(2,1)S(1)}, bf16[64,256]{1,0:T(8,128)(2,1)S(1)}, bf16[64,256]{1,0:T(8,128)(2,1)S(1)}, bf16[64,256]{1,0:T(8,128)(2,1)S(1)}) custom-call(f32[256,512]{1,0:T(8,128)S(1)} %get-tuple-element.21.mine_ref, f32[256,512]{1,0:T(8,128)S(1)} %collective-permute-done.1.other_ref, ...), custom_call_target="tpu_custom_call" | custom-call | flops 134217728 | bytes 1572864 | tf_op jit(solution)/shard_map/pallas_call | solution.py:134
  10.5 1.7 %collective-permute-start.2 = (bf16[64,256]{1,0:T(8,128)(2,1)S(1)}, bf16[64,256]{1,0:T(8,128)(2,1)S(1)}, u32[]{:S(2)}, u32[]{:S(2)}) collective-permute-start(bf16[64,256]{1,0:T(8,128)(2,1)S(1)} %get-tuple-element.26), channel_id=1, source_target_pairs={{0,4},{4,0},{8,12},{12,8},{1,5},{5,1},{9,13},{13,9},{2,6},{6,2},{1... | collective-permute-start | bytes 98312 | tf_op jit(solution)/shard_map/ppermute | solution.py:446
  12.1 2.6 %collective-permute-start.3 = (bf16[64,256]{1,0:T(8,128)(2,1)S(1)}, bf16[64,256]{1,0:T(8,128)(2,1)S(1)}, u32[]{:S(2)}, u32[]{:S(2)}) collective-permute-start(bf16[64,256]{1,0:T(8,128)(2,1)S(1)} %get-tuple-element.27), channel_id=1, source_target_pairs={{0,8},{4,12},{8,0},{12,4},{1,9},{5,13},{9,1},{13,5},{2,10},{6,14},... | collective-permute-start | bytes 98312 | tf_op jit(solution)/shard_map/ppermute | solution.py:446
  14.7 0.2 collective-permute-start.4
  15.0 1.7 %shard_map.77.refs_6_ = bf16[80,64,256]{2,1,0:T(8,128)(2,1)S(1)} custom-call(bf16[1280,64,256]{2,1,0:T(8,128)(2,1)} %refs_7_.3), custom_call_target="tpu_custom_call" | custom-call | bytes 2621440 | tf_op jit(solution)/shard_map/pallas_call | solution.py:154
  16.7 0.0 collective-permute-done.2.refs_1_
  16.7 0.9 %collective-permute-done.3.refs_2_ = bf16[64,256]{1,0:T(8,128)(2,1)S(1)} collective-permute-done((bf16[64,256]{1,0:T(8,128)(2,1)S(1)}, bf16[64,256]{1,0:T(8,128)(2,1)S(1)}, u32[]{:S(2)}, u32[]{:S(2)}) %collective-permute-start.3) | collective-permute-done | bytes 32800 | tf_op jit(solution)/shard_map/ppermute | solution.py:446
  17.6 2.9 %collective-permute-done.4.refs_3_ = bf16[64,256]{1,0:T(8,128)(2,1)S(1)} collective-permute-done((bf16[64,256]{1,0:T(8,128)(2,1)S(1)}, bf16[64,256]{1,0:T(8,128)(2,1)S(1)}, u32[]{:S(2)}, u32[]{:S(2)}) %collective-permute-start.4) | collective-permute-done | bytes 32800 | tf_op jit(solution)/shard_map/ppermute | solution.py:446
  20.4 0.0 copy-done
  20.4 0.6 %shard_map.76.tags_ref = bf16[144,256]{1,0:T(8,128)(2,1)S(1)} custom-call(s32[4]{0:T(128)S(1)} %copy-done, bf16[64,256]{1,0:T(8,128)(2,1)S(1)} %get-tuple-element.25.refs_0_, bf16[64,256]{1,0:T(8,128)(2,1)S(1)} %collective-permute-done.2.refs_1_, bf16[64,256]{1,0:T(8,128)(2,1)S(1)} %collective-permute-done.3.refs_2_, ...), custom_call_target="tpu_custom_call" | custom-call | bytes 262144 | tf_op jit(solution)/shard_map/pallas_call | solution.py:193
  21.0 1.6 %collective-permute-start.5 = (bf16[144,256]{1,0:T(8,128)(2,1)S(1)}, bf16[144,256]{1,0:T(8,128)(2,1)S(1)}, u32[]{:S(2)}, u32[]{:S(2)}) collective-permute-start(bf16[144,256]{1,0:T(8,128)(2,1)S(1)} %shard_map.76.tags_ref), channel_id=1, source_target_pairs={{0,16},{16,0},{1,17},{17,1},{2,18},{18,2},{3,19},{19,3},{4,20},{20... | collective-permute-start | bytes 221192 | tf_op jit(solution)/shard_map/ppermute | solution.py:449
  22.6 3.5 %shard_map.78 = (f32[16,320]{1,0:T(8,128)S(1)}, bf16[480,32,256]{2,1,0:T(8,128)(2,1)S(1)}) custom-call(bf16[144,256]{1,0:T(8,128)(2,1)S(1)} %shard_map.76.tags_ref, bf16[64,256]{1,0:T(8,128)(2,1)S(1)} %get-tuple-element.25.refs_0_, bf16[64,256]{1,0:T(8,128)(2,1)S(1)} %collective-permute-done.2.refs_1_, bf16[64,256]{1,0:T(8,128)(2,1)S(1)} %collective-permute-done.3.refs_2_, ...), custom_call_target="tpu_custom_call" | custom-call | flops 1342177280 | bytes 26214400 | tf_op jit(solution)/shard_map/pallas_call | solution.py:300
  26.1 0.0 collective-permute-done.5.refs_4_
  26.1 5.7 %shard_map.79 = f32[32,1,320]{2,1,0:T(1,128)S(1)} custom-call(bf16[144,256]{1,0:T(8,128)(2,1)S(1)} %shard_map.76.tags_ref, bf16[64,256]{1,0:T(8,128)(2,1)S(1)} %get-tuple-element.25.refs_0_, bf16[64,256]{1,0:T(8,128)(2,1)S(1)} %collective-permute-done.2.refs_1_, bf16[64,256]{1,0:T(8,128)(2,1)S(1)} %collective-permute-done.3.refs_2_, ...), custom_call_target="tpu_custom_call" | custom-call | flops 5368709120 | bytes 15728640 | tf_op jit(solution)/shard_map/pallas_call | solution.py:402
  31.8 9.0 %all_to_all.5 = f32[32,1,320]{2,1,0:T(1,128)S(1)} all-to-all(f32[32,1,320]{2,1,0:T(1,128)S(1)} %shard_map.79), channel_id=1, replica_groups=mesh['parts'=2,'wide'=4,'rep'=2,'sub'=2] {'parts','wide','rep','sub'}, dimensions={0} | all-to-all | bytes 81920 | tf_op jit(solution)/shard_map/all_to_all | solution.py:456
  40.8 0.1 reduce_sum.11
  40.9 0.6 %reduce_sum.12 = f32[1,320]{1,0:T(1,128)} reshape(f32[320]{0:T(512)S(1)} %reduce_sum.11) | data formatting | bytes 2560 | tf_op jit(solution)/shard_map/reduce_sum | solution.py:459
  (1 shorter events, 0.0 us)
Async XLA Ops:
  0.9 7.1 %collective-permute-start = (bf16[256,256]{1,0:T(8,128)(2,1)S(1)}, bf16[256,256]{1,0:T(8,128)(2,1)S(1)}, u32[]{:S(2)}, u32[]{:S(2)}) collective-permute-start(bf16[256,256]{1,0:T(8,128)(2,1)S(1)} %constant_dynamic-slice_fusion), channel_id=1, source_target_pairs={{0,2},{2,0},{1,3},{3,1},{4,6},{6,4},{5,7},{7,5},{8,10},{10,8},{9,1... | collective-permute-start | bytes 393224 | tf_op jit(solution)/shard_map/ppermute | solution.py:435
  8.0 2.0 %collective-permute-start.1 = (f32[256,512]{1,0:T(8,128)S(1)}, f32[256,512]{1,0:T(8,128)S(1)}, u32[]{:S(2)}, u32[]{:S(2)}) collective-permute-start(f32[256,512]{1,0:T(8,128)S(1)} %get-tuple-element.21.mine_ref), channel_id=1, source_target_pairs={{0,1},{1,0},{2,3},{3,2},{4,5},{5,4},{6,7},{7,6},{8,9},{9,8},{10,11... | collective-permute-start | bytes 1572872 | tf_op jit(solution)/shard_map/ppermute | solution.py:442
  10.5 6.2 %collective-permute-start.2 = (bf16[64,256]{1,0:T(8,128)(2,1)S(1)}, bf16[64,256]{1,0:T(8,128)(2,1)S(1)}, u32[]{:S(2)}, u32[]{:S(2)}) collective-permute-start(bf16[64,256]{1,0:T(8,128)(2,1)S(1)} %get-tuple-element.26), channel_id=1, source_target_pairs={{0,4},{4,0},{8,12},{12,8},{1,5},{5,1},{9,13},{13,9},{2,6},{6,2},{1... | collective-permute-start | bytes 98312 | tf_op jit(solution)/shard_map/ppermute | solution.py:446
  12.1 5.4 %collective-permute-start.3 = (bf16[64,256]{1,0:T(8,128)(2,1)S(1)}, bf16[64,256]{1,0:T(8,128)(2,1)S(1)}, u32[]{:S(2)}, u32[]{:S(2)}) collective-permute-start(bf16[64,256]{1,0:T(8,128)(2,1)S(1)} %get-tuple-element.27), channel_id=1, source_target_pairs={{0,8},{4,12},{8,0},{12,4},{1,9},{5,13},{9,1},{13,5},{2,10},{6,14},... | collective-permute-start | bytes 98312 | tf_op jit(solution)/shard_map/ppermute | solution.py:446
  14.7 5.7 %copy-start = (s32[4]{0:T(128)S(1)}, s32[4]{0:T(128)}, u32[]{:S(2)}) copy-start(s32[4]{0:T(128)} %order_ref.1) | copy-start | bytes 52
  14.7 5.7 %collective-permute-start.4 = (bf16[64,256]{1,0:T(8,128)(2,1)S(1)}, bf16[64,256]{1,0:T(8,128)(2,1)S(1)}, u32[]{:S(2)}, u32[]{:S(2)}) collective-permute-start(bf16[64,256]{1,0:T(8,128)(2,1)S(1)} %get-tuple-element.28), channel_id=1, source_target_pairs={{0,12},{4,8},{8,4},{12,0},{1,13},{5,9},{9,5},{13,1},{2,14},{6,10},... | collective-permute-start | bytes 98312 | tf_op jit(solution)/shard_map/ppermute | solution.py:446
  21.0 5.1 %collective-permute-start.5 = (bf16[144,256]{1,0:T(8,128)(2,1)S(1)}, bf16[144,256]{1,0:T(8,128)(2,1)S(1)}, u32[]{:S(2)}, u32[]{:S(2)}) collective-permute-start(bf16[144,256]{1,0:T(8,128)(2,1)S(1)} %shard_map.76.tags_ref), channel_id=1, source_target_pairs={{0,16},{16,0},{1,17},{17,1},{2,18},{18,2},{3,19},{19,3},{4,20},{20... | collective-permute-start | bytes 221192 | tf_op jit(solution)/shard_map/ppermute | solution.py:449

commit v4 on v3

--- a/solution.py
+++ b/solution.py
@@ -451,7 +451,7 @@
         parts, tagged, grads, [first, second, third], queries, later
     )
     partial = shared_scores(
-        parts, rep * sub, 3, tagged, grads, far, local, held, queries
+        parts, rep * sub, 2, tagged, grads, far, local, held, queries
     )
     gathered = lax.all_to_all(
         partial, ("parts", "wide", "rep", "sub"), split_axis=0, concat_axis=0, tiled=True

time: 41.7 us -> 41.3 us (level)
  no operation moved by 1% of the time
where the time goes in v4:
time: 41.3 us; the launch traced here: 41 us
  Pallas kernels  16.7 us (40%)
  starting transfers between devices  9.14 us (22%)
  blocking collectives  9.03 us (22%)
  waiting for transfers between devices  3.87 us (9%)
  local copies, waits for them, and re-layouts  1.48 us (4%)
  between operations  0.75 us (2%)
    all_to_all x1, blocking collectives, shared(): lax.all_to_all(partial, ('parts', 'wide', 'rep', 'sub'), split_axis=0, co...  9.03 us
    pallas_call x1, Pallas kernels, shared_scores(): pl.pallas_call(functools.partial(shared_score_kernel, wide, pieces), out_...  5.27 us
    ppermute x3, starting transfers between devices, shared(): lax.ppermute(sent[k], 'wide', [(i, i ^ k) for i in range(wide)])  4.48 us
    ppermute x3, waiting for transfers between devices, shared(): lax.ppermute(sent[k], 'wide', [(i, i ^ k) for i in range(wide)])  3.73 us
    pallas_call x2, Pallas kernels, fetch(): pl.pallas_call(functools.partial(fetch_kernel, first), out_shape=pltpu.VM...  3.5 us
    pallas_call x1, Pallas kernels, local_scores(): pl.pallas_call(functools.partial(local_score_kernel, wide, len(here)), ou...  3.48 us
    pallas_call x1, Pallas kernels, row_product(): pl.pallas_call(row_product_kernel, out_shape=(jax.ShapeDtypeStruct((rows,...  3.45 us
    ppermute x1, starting transfers between devices, shared(): far_block = lax.ppermute(own_block, 'rep', [(0, 1), (1, 0)])  3 us
  transfers between devices with their start and end apart: 6, of which 3 were waited for; matrix products, arithmetic and copies ran while one was open for 0% of the time, Pallas kernels for 25%

profile of v4, /device:TPU:0, one launch (start us, length us, event | category | flops | bytes accessed | tf_op | source)
XLA Modules:
  0.0 41.0 jit_solution(13340709856809019195)
XLA Ops:
  0.0 0.9 %constant_dynamic-slice_fusion = bf16[256,256]{1,0:T(8,128)(2,1)S(1)} fusion(bf16[512,256]{1,0:T(8,128)(2,1)} %col_factor_ref.1, s32[]{:T(128)S(6)} %select_n.3), kind=kLoop, calls=%fused_computation | loop fusion | bytes 262148 | tf_op jit(solution)/shard_map/dynamic_slice | solution.py:434
  0.9 3.0 %collective-permute-start = (bf16[256,256]{1,0:T(8,128)(2,1)S(1)}, bf16[256,256]{1,0:T(8,128)(2,1)S(1)}, u32[]{:S(2)}, u32[]{:S(2)}) collective-permute-start(bf16[256,256]{1,0:T(8,128)(2,1)S(1)} %constant_dynamic-slice_fusion), channel_id=1, source_target_pairs={{0,2},{2,0},{1,3},{3,1},{4,6},{6,4},{5,7},{7,5},{8,10},{10,8},{9,1... | collective-permute-start | bytes 393224 | tf_op jit(solution)/shard_map/ppermute | solution.py:435
  4.6 3.4 %shard_map.73 = (f32[256,512]{1,0:T(8,128)S(1)}, bf16[512,256]{1,0:T(8,128)(2,1)S(1)}, bf16[160,64,256]{2,1,0:T(8,128)(2,1)S(1)}) custom-call(s32[1]{0:T(128)S(6)} %copy.8.pad_ref, bf16[1024,512]{1,0:T(8,128)(2,1)} %bitcast.2, bf16[1024,512]{1,0:T(8,128)(2,1)} %bitcast.3, bf16[512,256]{1,0:T(8,128)(2,1)} %row_factor_ref.1, bf16[512,256]{1,0:T(8,128)(2,1)} %col_factor_ref.1, ...), custom_call_target="tpu_custom_call" | custom-call | flops 536870912 | bytes 2097152 | tf_op jit(solution)/shard_map/pallas_call | solution.py:72
  8.0 0.0 collective-permute-done.far_ref
  8.0 0.1 collective-permute-start.1
  8.1 1.8 %shard_map.74.refs_5_ = bf16[80,64,256]{2,1,0:T(8,128)(2,1)S(1)} custom-call(bf16[1280,64,256]{2,1,0:T(8,128)(2,1)} %refs_7_.3), custom_call_target="tpu_custom_call" | custom-call | bytes 2621440 | tf_op jit(solution)/shard_map/pallas_call | solution.py:154
  9.9 0.1 collective-permute-done.1.other_ref
  10.0 0.5 %shard_map.75 = (bf16[64,256]{1,0:T(8,128)(2,1)S(1)}, bf16[64,256]{1,0:T(8,128)(2,1)S(1)}, bf16[64,256]{1,0:T(8,128)(2,1)S(1)}, bf16[64,256]{1,0:T(8,128)(2,1)S(1)}) custom-call(f32[256,512]{1,0:T(8,128)S(1)} %get-tuple-element.21.mine_ref, f32[256,512]{1,0:T(8,128)S(1)} %collective-permute-done.1.other_ref, ...), custom_call_target="tpu_custom_call" | custom-call | flops 134217728 | bytes 1572864 | tf_op jit(solution)/shard_map/pallas_call | solution.py:134
  10.5 1.7 %collective-permute-start.2 = (bf16[64,256]{1,0:T(8,128)(2,1)S(1)}, bf16[64,256]{1,0:T(8,128)(2,1)S(1)}, u32[]{:S(2)}, u32[]{:S(2)}) collective-permute-start(bf16[64,256]{1,0:T(8,128)(2,1)S(1)} %get-tuple-element.26), channel_id=1, source_target_pairs={{0,4},{4,0},{8,12},{12,8},{1,5},{5,1},{9,13},{13,9},{2,6},{6,2},{1... | collective-permute-start | bytes 98312 | tf_op jit(solution)/shard_map/ppermute | solution.py:446
  12.1 2.6 %collective-permute-start.3 = (bf16[64,256]{1,0:T(8,128)(2,1)S(1)}, bf16[64,256]{1,0:T(8,128)(2,1)S(1)}, u32[]{:S(2)}, u32[]{:S(2)}) collective-permute-start(bf16[64,256]{1,0:T(8,128)(2,1)S(1)} %get-tuple-element.27), channel_id=1, source_target_pairs={{0,8},{4,12},{8,0},{12,4},{1,9},{5,13},{9,1},{13,5},{2,10},{6,14},... | collective-permute-start | bytes 98312 | tf_op jit(solution)/shard_map/ppermute | solution.py:446
  14.7 0.2 collective-permute-start.4
  15.0 1.7 %shard_map.77.refs_6_ = bf16[80,64,256]{2,1,0:T(8,128)(2,1)S(1)} custom-call(bf16[1280,64,256]{2,1,0:T(8,128)(2,1)} %refs_7_.3), custom_call_target="tpu_custom_call" | custom-call | bytes 2621440 | tf_op jit(solution)/shard_map/pallas_call | solution.py:154
  16.7 0.0 collective-permute-done.2.refs_1_
  16.7 0.9 %collective-permute-done.3.refs_2_ = bf16[64,256]{1,0:T(8,128)(2,1)S(1)} collective-permute-done((bf16[64,256]{1,0:T(8,128)(2,1)S(1)}, bf16[64,256]{1,0:T(8,128)(2,1)S(1)}, u32[]{:S(2)}, u32[]{:S(2)}) %collective-permute-start.3) | collective-permute-done | bytes 32800 | tf_op jit(solution)/shard_map/ppermute | solution.py:446
  17.6 2.9 %collective-permute-done.4.refs_3_ = bf16[64,256]{1,0:T(8,128)(2,1)S(1)} collective-permute-done((bf16[64,256]{1,0:T(8,128)(2,1)S(1)}, bf16[64,256]{1,0:T(8,128)(2,1)S(1)}, u32[]{:S(2)}, u32[]{:S(2)}) %collective-permute-start.4) | collective-permute-done | bytes 32800 | tf_op jit(solution)/shard_map/ppermute | solution.py:446
  20.4 0.0 copy-done
  20.4 0.6 %shard_map.76.tags_ref = bf16[144,256]{1,0:T(8,128)(2,1)S(1)} custom-call(s32[4]{0:T(128)S(1)} %copy-done, bf16[64,256]{1,0:T(8,128)(2,1)S(1)} %get-tuple-element.25.refs_0_, bf16[64,256]{1,0:T(8,128)(2,1)S(1)} %collective-permute-done.2.refs_1_, bf16[64,256]{1,0:T(8,128)(2,1)S(1)} %collective-permute-done.3.refs_2_, ...), custom_call_target="tpu_custom_call" | custom-call | bytes 262144 | tf_op jit(solution)/shard_map/pallas_call | solution.py:193
  21.0 1.6 %collective-permute-start.5 = (bf16[144,256]{1,0:T(8,128)(2,1)S(1)}, bf16[144,256]{1,0:T(8,128)(2,1)S(1)}, u32[]{:S(2)}, u32[]{:S(2)}) collective-permute-start(bf16[144,256]{1,0:T(8,128)(2,1)S(1)} %shard_map.76.tags_ref), channel_id=1, source_target_pairs={{0,16},{16,0},{1,17},{17,1},{2,18},{18,2},{3,19},{19,3},{4,20},{20... | collective-permute-start | bytes 221192 | tf_op jit(solution)/shard_map/ppermute | solution.py:449
  22.6 3.5 %shard_map.78 = (f32[16,320]{1,0:T(8,128)S(1)}, bf16[480,32,256]{2,1,0:T(8,128)(2,1)S(1)}) custom-call(bf16[144,256]{1,0:T(8,128)(2,1)S(1)} %shard_map.76.tags_ref, bf16[64,256]{1,0:T(8,128)(2,1)S(1)} %get-tuple-element.25.refs_0_, bf16[64,256]{1,0:T(8,128)(2,1)S(1)} %collective-permute-done.2.refs_1_, bf16[64,256]{1,0:T(8,128)(2,1)S(1)} %collective-permute-done.3.refs_2_, ...), custom_call_target="tpu_custom_call" | custom-call | flops 1342177280 | bytes 26214400 | tf_op jit(solution)/shard_map/pallas_call | solution.py:300
  26.1 0.0 collective-permute-done.5.refs_4_
  26.1 5.3 %shard_map.79 = f32[32,1,320]{2,1,0:T(1,128)S(1)} custom-call(bf16[144,256]{1,0:T(8,128)(2,1)S(1)} %shard_map.76.tags_ref, bf16[64,256]{1,0:T(8,128)(2,1)S(1)} %get-tuple-element.25.refs_0_, bf16[64,256]{1,0:T(8,128)(2,1)S(1)} %collective-permute-done.2.refs_1_, bf16[64,256]{1,0:T(8,128)(2,1)S(1)} %collective-permute-done.3.refs_2_, ...), custom_call_target="tpu_custom_call" | custom-call | flops 5368709120 | bytes 15728640 | tf_op jit(solution)/shard_map/pallas_call | solution.py:402
  31.4 9.0 %all_to_all.5 = f32[32,1,320]{2,1,0:T(1,128)S(1)} all-to-all(f32[32,1,320]{2,1,0:T(1,128)S(1)} %shard_map.79), channel_id=1, replica_groups=mesh['parts'=2,'wide'=4,'rep'=2,'sub'=2] {'parts','wide','rep','sub'}, dimensions={0} | all-to-all | bytes 81920 | tf_op jit(solution)/shard_map/all_to_all | solution.py:456
  40.4 0.1 reduce_sum.11
  40.5 0.6 %reduce_sum.12 = f32[1,320]{1,0:T(1,128)} reshape(f32[320]{0:T(512)S(1)} %reduce_sum.11) | data formatting | bytes 2560 | tf_op jit(solution)/shard_map/reduce_sum | solution.py:459
  (1 shorter events, 0.0 us)
Async XLA Ops:
  0.9 7.1 %collective-permute-start = (bf16[256,256]{1,0:T(8,128)(2,1)S(1)}, bf16[256,256]{1,0:T(8,128)(2,1)S(1)}, u32[]{:S(2)}, u32[]{:S(2)}) collective-permute-start(bf16[256,256]{1,0:T(8,128)(2,1)S(1)} %constant_dynamic-slice_fusion), channel_id=1, source_target_pairs={{0,2},{2,0},{1,3},{3,1},{4,6},{6,4},{5,7},{7,5},{8,10},{10,8},{9,1... | collective-permute-start | bytes 393224 | tf_op jit(solution)/shard_map/ppermute | solution.py:435
  8.0 2.0 %collective-permute-start.1 = (f32[256,512]{1,0:T(8,128)S(1)}, f32[256,512]{1,0:T(8,128)S(1)}, u32[]{:S(2)}, u32[]{:S(2)}) collective-permute-start(f32[256,512]{1,0:T(8,128)S(1)} %get-tuple-element.21.mine_ref), channel_id=1, source_target_pairs={{0,1},{1,0},{2,3},{3,2},{4,5},{5,4},{6,7},{7,6},{8,9},{9,8},{10,11... | collective-permute-start | bytes 1572872 | tf_op jit(solution)/shard_map/ppermute | solution.py:442
  10.5 6.2 %collective-permute-start.2 = (bf16[64,256]{1,0:T(8,128)(2,1)S(1)}, bf16[64,256]{1,0:T(8,128)(2,1)S(1)}, u32[]{:S(2)}, u32[]{:S(2)}) collective-permute-start(bf16[64,256]{1,0:T(8,128)(2,1)S(1)} %get-tuple-element.26), channel_id=1, source_target_pairs={{0,4},{4,0},{8,12},{12,8},{1,5},{5,1},{9,13},{13,9},{2,6},{6,2},{1... | collective-permute-start | bytes 98312 | tf_op jit(solution)/shard_map/ppermute | solution.py:446
  12.1 5.4 %collective-permute-start.3 = (bf16[64,256]{1,0:T(8,128)(2,1)S(1)}, bf16[64,256]{1,0:T(8,128)(2,1)S(1)}, u32[]{:S(2)}, u32[]{:S(2)}) collective-permute-start(bf16[64,256]{1,0:T(8,128)(2,1)S(1)} %get-tuple-element.27), channel_id=1, source_target_pairs={{0,8},{4,12},{8,0},{12,4},{1,9},{5,13},{9,1},{13,5},{2,10},{6,14},... | collective-permute-start | bytes 98312 | tf_op jit(solution)/shard_map/ppermute | solution.py:446
  14.7 5.7 %copy-start = (s32[4]{0:T(128)S(1)}, s32[4]{0:T(128)}, u32[]{:S(2)}) copy-start(s32[4]{0:T(128)} %order_ref.1) | copy-start | bytes 52
  14.7 5.7 %collective-permute-start.4 = (bf16[64,256]{1,0:T(8,128)(2,1)S(1)}, bf16[64,256]{1,0:T(8,128)(2,1)S(1)}, u32[]{:S(2)}, u32[]{:S(2)}) collective-permute-start(bf16[64,256]{1,0:T(8,128)(2,1)S(1)} %get-tuple-element.28), channel_id=1, source_target_pairs={{0,12},{4,8},{8,4},{12,0},{1,13},{5,9},{9,5},{13,1},{2,14},{6,10},... | collective-permute-start | bytes 98312 | tf_op jit(solution)/shard_map/ppermute | solution.py:446
  21.0 5.1 %collective-permute-start.5 = (bf16[144,256]{1,0:T(8,128)(2,1)S(1)}, bf16[144,256]{1,0:T(8,128)(2,1)S(1)}, u32[]{:S(2)}, u32[]{:S(2)}) collective-permute-start(bf16[144,256]{1,0:T(8,128)(2,1)S(1)} %shard_map.76.tags_ref), channel_id=1, source_target_pairs={{0,16},{16,0},{1,17},{17,1},{2,18},{18,2},{3,19},{19,3},{4,20},{20... | collective-permute-start | bytes 221192 | tf_op jit(solution)/shard_map/ppermute | solution.py:449

commit v5 on v4

--- a/solution.py
+++ b/solution.py
@@ -166,41 +166,67 @@
     )(pltpu.with_memory_space_constraint(queries, pltpu.HBM))
 
 
-def exchange_kernel(wide, order_ref, *refs):
-    grads, (out_ref, order, sem) = refs[:wide], refs[wide:]
-    rows, width = grads[0].shape
-    part, parts = lax.axis_index("parts"), lax.axis_size("parts")
-    share = rows // parts
-    copy = pltpu.make_async_copy(order_ref, order, sem)
+def tagged_fetch_kernel(first, wide, order_ref, queries_ref, out_ref, tags_ref, order, sems):
+    order_copy = pltpu.make_async_copy(order_ref, order, sems.at[0])
+    order_copy.start()
+    copy = pltpu.make_async_copy(
+        queries_ref.at[pl.ds(first, out_ref.shape[0])], out_ref, sems.at[1]
+    )
     copy.start()
-    first = pl.multiple_of((1 - part) * share, share)
+    order_copy.wait()
+    row = lax.broadcasted_iota(jnp.int32, tags_ref.shape, 0)
+    lane = lax.broadcasted_iota(jnp.int32, tags_ref.shape, 1)
+    tags = jnp.zeros(tags_ref.shape, F32)
+    for k in range(wide):
+        goal = lax.axis_index("parts") * wide + order[lax.axis_index("wide") ^ k]
+        tags += jnp.where((row == k) & (lane == goal), 1.0, 0.0)
+    tags_ref[...] = tags.astype(BF16)
+    copy.wait()
+
+
+def tagged_fetch(wide, order, queries, first, count):
+    width = queries.shape[2]
+    vmem = pl.BlockSpec(memory_space=pltpu.VMEM)
+    return pl.pallas_call(
+        functools.partial(tagged_fetch_kernel, first, wide),
+        out_shape=(
+            pltpu.VMEM((count,) + queries.shape[1:], BF16),
+            jax.ShapeDtypeStruct((GROUP, width), BF16),
+        ),
+        in_specs=[pl.BlockSpec(memory_space=pl.ANY), pl.BlockSpec(memory_space=pltpu.HBM)],
+        out_specs=(vmem, vmem),
+        scratch_shapes=[pltpu.SMEM(order.shape, jnp.int32), pltpu.SemaphoreType.DMA((2,))],
+        compiler_params=pltpu.CompilerParams(vmem_limit_bytes=2 << 20),
+        cost_estimate=pl.CostEstimate(
+            flops=0, bytes_accessed=2 * count * queries.shape[1] * width, transcendentals=0
+        ),
+    )(order, pltpu.with_memory_space_constraint(queries, pltpu.HBM))
+
+
+def exchange_kernel(wide, tags_ref, *refs):
+    grads, out_ref = refs[:wide], refs[wide]
+    rows = grads[0].shape[0]
+    share = rows // lax.axis_size("parts")
+    first = pl.multiple_of((1 - lax.axis_index("parts")) * share, share)
     for k in range(wide):
         out_ref[k * share : (k + 1) * share, :] = grads[k][pl.ds(first, share), :]
-    copy.wait()
-    row = lax.broadcasted_iota(jnp.int32, (GROUP, width), 0)
-    lane = lax.broadcasted_iota(jnp.int32, (GROUP, width), 1)
-    tags = jnp.zeros((GROUP, width), F32)
-    for k in range(wide):
-        goal = part * wide + order[lax.axis_index("wide") ^ k]
-        tags += jnp.where((row == k) & (lane == goal), 1.0, 0.0)
-    out_ref[wide * share :, :] = tags.astype(BF16)
-
-
-def exchange_block(parts, order, grads):
+    out_ref[wide * share :, :] = tags_ref[...]
+
+
+def exchange_block(parts, tags, grads):
     wide = len(grads)
     rows, width = grads[0].shape
     vmem = pl.BlockSpec(memory_space=pltpu.VMEM)
     return pl.pallas_call(
         functools.partial(exchange_kernel, wide),
         out_shape=jax.ShapeDtypeStruct((wide * rows // parts + GROUP, width), BF16),
-        in_specs=[pl.BlockSpec(memory_space=pl.ANY)] + [vmem] * wide,
+        in_specs=[vmem] * (wide + 1),
         out_specs=vmem,
-        scratch_shapes=[pltpu.SMEM(order.shape, jnp.int32), pltpu.SemaphoreType.DMA],
         compiler_params=pltpu.CompilerParams(vmem_limit_bytes=2 << 20),
         cost_estimate=pl.CostEstimate(
             flops=0, bytes_accessed=4 * wide * rows * width, transcendentals=0
         ),
-    )(order, *grads)
+    )(tags, *grads)
 
 
 def joined_rows(source, first, count, start, rows):
@@ -437,7 +463,7 @@
         padding, deltas[0], activations[0], delta_factor, act_factor, queries, early
     )
     second = fetch(queries, early, early // 2)
-    third = fetch(queries, 3 * early // 2, early // 2)
+    third, tags = tagged_fetch(wide, assignment, queries, 3 * early // 2, early // 2)
     mine, columns, far_block = lax.optimization_barrier((mine, columns, far_block))
     other = lax.ppermute(mine, "sub", [(0, 1), (1, 0)])
     other, second = lax.optimization_barrier((other, second))
@@ -445,7 +471,7 @@
     grads = [sent[0]] + [
         lax.ppermute(sent[k], "wide", [(i, i ^ k) for i in range(wide)]) for k in range(1, wide)
     ]
-    tagged = exchange_block(parts, assignment, grads)
+    tagged = exchange_block(parts, tags, grads)
     far = lax.ppermute(tagged, "parts", [(0, 1), (1, 0)])
     local, held = local_scores(
         parts, tagged, grads, [first, second, third], queries, later

time: 41.3 us -> 40.6 us (0.983)
  Pallas kernels: 16.7 us -> 16.1 us
    pallas_call x0 -> x1, Pallas kernels: none -> 1.76 us  [tagged_fetch(): pl.pallas_call(functools.partial(tagged_fetch_kernel, first, wide), out_s...]
    pallas_call x2 -> x1, Pallas kernels: 3.5 us -> 1.75 us  [fetch(): pl.pallas_call(functools.partial(fetch_kernel, first), out_shape=pltpu.VM...]
    pallas_call x1, Pallas kernels: 0.56 us -> 0.01 us  [exchange_block(): pl.pallas_call(functools.partial(exchange_kernel, wide), out_shape=jax.Sh...]
  transfers between devices with their start and end apart: 6 -> 6, of which waited for: 3 -> 3; matrix products, arithmetic and copies ran while one was open for 0% -> 0% of each run, Pallas kernels for 25% -> 26%
where the time goes in v5:
time: 40.6 us; the launch traced here: 40.3 us
  Pallas kernels  16.1 us (40%)
  starting transfers between devices  9.07 us (22%)
  blocking collectives  9.03 us (22%)
  waiting for transfers between devices  3.86 us (10%)
  local copies, waits for them, and re-layouts  1.49 us (4%)
  between operations  0.75 us (2%)
    all_to_all x1, blocking collectives, shared(): lax.all_to_all(partial, ('parts', 'wide', 'rep', 'sub'), split_axis=0, co...  9.03 us
    pallas_call x1, Pallas kernels, shared_scores(): pl.pallas_call(functools.partial(shared_score_kernel, wide, pieces), out_...  5.26 us
    ppermute x3, starting transfers between devices, shared(): lax.ppermute(sent[k], 'wide', [(i, i ^ k) for i in range(wide)])  4.48 us
    ppermute x3, waiting for transfers between devices, shared(): lax.ppermute(sent[k], 'wide', [(i, i ^ k) for i in range(wide)])  3.71 us
    pallas_call x1, Pallas kernels, row_product(): pl.pallas_call(row_product_kernel, out_shape=(jax.ShapeDtypeStruct((rows,...  3.45 us
    pallas_call x1, Pallas kernels, local_scores(): pl.pallas_call(functools.partial(local_score_kernel, wide, len(here)), ou...  3.42 us
    ppermute x1, starting transfers between devices, shared(): far_block = lax.ppermute(own_block, 'rep', [(0, 1), (1, 0)])  3 us
    pallas_call x1, Pallas kernels, tagged_fetch(): pl.pallas_call(functools.partial(tagged_fetch_kernel, first, wide), out_s...  1.76 us
  transfers between devices with their start and end apart: 6, of which 3 were waited for; matrix products, arithmetic and copies ran while one was open for 0% of the time, Pallas kernels for 26%

profile of v5, /device:TPU:0, one launch (start us, length us, event | category | flops | bytes accessed | tf_op | source)
XLA Modules:
  0.0 40.3 jit_solution(16828142099683113863)
XLA Ops:
  0.0 0.9 %constant_dynamic-slice_fusion = bf16[256,256]{1,0:T(8,128)(2,1)S(1)} fusion(bf16[512,256]{1,0:T(8,128)(2,1)} %col_factor_ref.1, s32[]{:T(128)S(6)} %select_n.3), kind=kLoop, calls=%fused_computation | loop fusion | bytes 262148 | tf_op jit(solution)/shard_map/dynamic_slice | solution.py:460
  0.9 3.0 %collective-permute-start = (bf16[256,256]{1,0:T(8,128)(2,1)S(1)}, bf16[256,256]{1,0:T(8,128)(2,1)S(1)}, u32[]{:S(2)}, u32[]{:S(2)}) collective-permute-start(bf16[256,256]{1,0:T(8,128)(2,1)S(1)} %constant_dynamic-slice_fusion), channel_id=1, source_target_pairs={{0,2},{2,0},{1,3},{3,1},{4,6},{6,4},{5,7},{7,5},{8,10},{10,8},{9,1... | collective-permute-start | bytes 393224 | tf_op jit(solution)/shard_map/ppermute | solution.py:461
  4.6 3.4 %shard_map.74 = (f32[256,512]{1,0:T(8,128)S(1)}, bf16[512,256]{1,0:T(8,128)(2,1)S(1)}, bf16[160,64,256]{2,1,0:T(8,128)(2,1)S(1)}) custom-call(s32[1]{0:T(128)S(6)} %copy.8.pad_ref, bf16[1024,512]{1,0:T(8,128)(2,1)} %bitcast.2, bf16[1024,512]{1,0:T(8,128)(2,1)} %bitcast.3, bf16[512,256]{1,0:T(8,128)(2,1)} %row_factor_ref.1, bf16[512,256]{1,0:T(8,128)(2,1)} %col_factor_ref.1, ...), custom_call_target="tpu_custom_call" | custom-call | flops 536870912 | bytes 2097152 | tf_op jit(solution)/shard_map/pallas_call | solution.py:72
  8.0 0.0 collective-permute-done.far_ref
  8.0 0.0 copy-start
  8.0 0.1 collective-permute-start.1
  8.1 1.8 %shard_map.75.refs_5_ = bf16[80,64,256]{2,1,0:T(8,128)(2,1)S(1)} custom-call(bf16[1280,64,256]{2,1,0:T(8,128)(2,1)} %refs_7_.3), custom_call_target="tpu_custom_call" | custom-call | bytes 2621440 | tf_op jit(solution)/shard_map/pallas_call | solution.py:154
  9.9 0.1 collective-permute-done.1.other_ref
  10.0 0.5 %shard_map.76 = (bf16[64,256]{1,0:T(8,128)(2,1)S(1)}, bf16[64,256]{1,0:T(8,128)(2,1)S(1)}, bf16[64,256]{1,0:T(8,128)(2,1)S(1)}, bf16[64,256]{1,0:T(8,128)(2,1)S(1)}) custom-call(f32[256,512]{1,0:T(8,128)S(1)} %get-tuple-element.24.mine_ref, f32[256,512]{1,0:T(8,128)S(1)} %collective-permute-done.1.other_ref, ...), custom_call_target="tpu_custom_call" | custom-call | flops 134217728 | bytes 1572864 | tf_op jit(solution)/shard_map/pallas_call | solution.py:134
  10.5 1.7 %collective-permute-start.2 = (bf16[64,256]{1,0:T(8,128)(2,1)S(1)}, bf16[64,256]{1,0:T(8,128)(2,1)S(1)}, u32[]{:S(2)}, u32[]{:S(2)}) collective-permute-start(bf16[64,256]{1,0:T(8,128)(2,1)S(1)} %get-tuple-element.29), channel_id=1, source_target_pairs={{0,4},{4,0},{8,12},{12,8},{1,5},{5,1},{9,13},{13,9},{2,6},{6,2},{1... | collective-permute-start | bytes 98312 | tf_op jit(solution)/shard_map/ppermute | solution.py:472
  12.1 2.6 %collective-permute-start.3 = (bf16[64,256]{1,0:T(8,128)(2,1)S(1)}, bf16[64,256]{1,0:T(8,128)(2,1)S(1)}, u32[]{:S(2)}, u32[]{:S(2)}) collective-permute-start(bf16[64,256]{1,0:T(8,128)(2,1)S(1)} %get-tuple-element.30), channel_id=1, source_target_pairs={{0,8},{4,12},{8,0},{12,4},{1,9},{5,13},{9,1},{13,5},{2,10},{6,14},... | collective-permute-start | bytes 98312 | tf_op jit(solution)/shard_map/ppermute | solution.py:472
  14.7 0.2 collective-permute-start.4
  15.0 0.0 copy-done
  15.0 1.8 %shard_map.73 = (bf16[80,64,256]{2,1,0:T(8,128)(2,1)S(1)}, bf16[16,256]{1,0:T(8,128)(2,1)S(1)}) custom-call(s32[4]{0:T(128)S(1)} %copy-done, bf16[1280,64,256]{2,1,0:T(8,128)(2,1)} %refs_7_.3), custom_call_target="tpu_custom_call" | custom-call | bytes 2621440 | tf_op jit(solution)/shard_map/pallas_call | solution.py:190
  16.7 0.0 collective-permute-done.2.refs_1_
  16.7 0.9 %collective-permute-done.3.refs_2_ = bf16[64,256]{1,0:T(8,128)(2,1)S(1)} collective-permute-done((bf16[64,256]{1,0:T(8,128)(2,1)S(1)}, bf16[64,256]{1,0:T(8,128)(2,1)S(1)}, u32[]{:S(2)}, u32[]{:S(2)}) %collective-permute-start.3) | collective-permute-done | bytes 32800 | tf_op jit(solution)/shard_map/ppermute | solution.py:472
  17.6 2.9 %collective-permute-done.4.refs_3_ = bf16[64,256]{1,0:T(8,128)(2,1)S(1)} collective-permute-done((bf16[64,256]{1,0:T(8,128)(2,1)S(1)}, bf16[64,256]{1,0:T(8,128)(2,1)S(1)}, u32[]{:S(2)}, u32[]{:S(2)}) %collective-permute-start.4) | collective-permute-done | bytes 32800 | tf_op jit(solution)/shard_map/ppermute | solution.py:472
  20.5 1.5 %collective-permute-start.5 = (bf16[144,256]{1,0:T(8,128)(2,1)S(1)}, bf16[144,256]{1,0:T(8,128)(2,1)S(1)}, u32[]{:S(2)}, u32[]{:S(2)}) collective-permute-start(bf16[144,256]{1,0:T(8,128)(2,1)S(1)} %shard_map.77.tags_ref), channel_id=1, source_target_pairs={{0,16},{16,0},{1,17},{17,1},{2,18},{18,2},{3,19},{19,3},{4,20},{20... | collective-permute-start | bytes 221192 | tf_op jit(solution)/shard_map/ppermute | solution.py:475
  22.0 3.4 %shard_map.78 = (f32[16,320]{1,0:T(8,128)S(1)}, bf16[480,32,256]{2,1,0:T(8,128)(2,1)S(1)}) custom-call(bf16[144,256]{1,0:T(8,128)(2,1)S(1)} %shard_map.77.tags_ref, bf16[64,256]{1,0:T(8,128)(2,1)S(1)} %get-tuple-element.28.refs_0_, bf16[64,256]{1,0:T(8,128)(2,1)S(1)} %collective-permute-done.2.refs_1_, bf16[64,256]{1,0:T(8,128)(2,1)S(1)} %collective-permute-done.3.refs_2_, ...), custom_call_target="tpu_custom_call" | custom-call | flops 1342177280 | bytes 26214400 | tf_op jit(solution)/shard_map/pallas_call | solution.py:326
  25.4 0.0 collective-permute-done.5.refs_4_
  25.4 5.3 %shard_map.79 = f32[32,1,320]{2,1,0:T(1,128)S(1)} custom-call(bf16[144,256]{1,0:T(8,128)(2,1)S(1)} %shard_map.77.tags_ref, bf16[64,256]{1,0:T(8,128)(2,1)S(1)} %get-tuple-element.28.refs_0_, bf16[64,256]{1,0:T(8,128)(2,1)S(1)} %collective-permute-done.2.refs_1_, bf16[64,256]{1,0:T(8,128)(2,1)S(1)} %collective-permute-done.3.refs_2_, ...), custom_call_target="tpu_custom_call" | custom-call | flops 5368709120 | bytes 15728640 | tf_op jit(solution)/shard_map/pallas_call | solution.py:428
  30.7 9.0 %all_to_all.5 = f32[32,1,320]{2,1,0:T(1,128)S(1)} all-to-all(f32[32,1,320]{2,1,0:T(1,128)S(1)} %shard_map.79), channel_id=1, replica_groups=mesh['parts'=2,'wide'=4,'rep'=2,'sub'=2] {'parts','wide','rep','sub'}, dimensions={0} | all-to-all | bytes 81920 | tf_op jit(solution)/shard_map/all_to_all | solution.py:482
  39.7 0.1 reduce_sum.11
  39.8 0.6 %reduce_sum.12 = f32[1,320]{1,0:T(1,128)} reshape(f32[320]{0:T(512)S(1)} %reduce_sum.11) | data formatting | bytes 2560 | tf_op jit(solution)/shard_map/reduce_sum | solution.py:485
  (1 shorter events, 0.0 us)
Async XLA Ops:
  0.9 7.1 %collective-permute-start = (bf16[256,256]{1,0:T(8,128)(2,1)S(1)}, bf16[256,256]{1,0:T(8,128)(2,1)S(1)}, u32[]{:S(2)}, u32[]{:S(2)}) collective-permute-start(bf16[256,256]{1,0:T(8,128)(2,1)S(1)} %constant_dynamic-slice_fusion), channel_id=1, source_target_pairs={{0,2},{2,0},{1,3},{3,1},{4,6},{6,4},{5,7},{7,5},{8,10},{10,8},{9,1... | collective-permute-start | bytes 393224 | tf_op jit(solution)/shard_map/ppermute | solution.py:461
  8.0 6.9 %copy-start = (s32[4]{0:T(128)S(1)}, s32[4]{0:T(128)}, u32[]{:S(2)}) copy-start(s32[4]{0:T(128)} %order_ref.1) | copy-start | bytes 52
  8.0 2.0 %collective-permute-start.1 = (f32[256,512]{1,0:T(8,128)S(1)}, f32[256,512]{1,0:T(8,128)S(1)}, u32[]{:S(2)}, u32[]{:S(2)}) collective-permute-start(f32[256,512]{1,0:T(8,128)S(1)} %get-tuple-element.24.mine_ref), channel_id=1, source_target_pairs={{0,1},{1,0},{2,3},{3,2},{4,5},{5,4},{6,7},{7,6},{8,9},{9,8},{10,11... | collective-permute-start | bytes 1572872 | tf_op jit(solution)/shard_map/ppermute | solution.py:468
  10.5 6.2 %collective-permute-start.2 = (bf16[64,256]{1,0:T(8,128)(2,1)S(1)}, bf16[64,256]{1,0:T(8,128)(2,1)S(1)}, u32[]{:S(2)}, u32[]{:S(2)}) collective-permute-start(bf16[64,256]{1,0:T(8,128)(2,1)S(1)} %get-tuple-element.29), channel_id=1, source_target_pairs={{0,4},{4,0},{8,12},{12,8},{1,5},{5,1},{9,13},{13,9},{2,6},{6,2},{1... | collective-permute-start | bytes 98312 | tf_op jit(solution)/shard_map/ppermute | solution.py:472
  12.1 5.4 %collective-permute-start.3 = (bf16[64,256]{1,0:T(8,128)(2,1)S(1)}, bf16[64,256]{1,0:T(8,128)(2,1)S(1)}, u32[]{:S(2)}, u32[]{:S(2)}) collective-permute-start(bf16[64,256]{1,0:T(8,128)(2,1)S(1)} %get-tuple-element.30), channel_id=1, source_target_pairs={{0,8},{4,12},{8,0},{12,4},{1,9},{5,13},{9,1},{13,5},{2,10},{6,14},... | collective-permute-start | bytes 98312 | tf_op jit(solution)/shard_map/ppermute | solution.py:472
  14.7 5.7 %collective-permute-start.4 = (bf16[64,256]{1,0:T(8,128)(2,1)S(1)}, bf16[64,256]{1,0:T(8,128)(2,1)S(1)}, u32[]{:S(2)}, u32[]{:S(2)}) collective-permute-start(bf16[64,256]{1,0:T(8,128)(2,1)S(1)} %get-tuple-element.31), channel_id=1, source_target_pairs={{0,12},{4,8},{8,4},{12,0},{1,13},{5,9},{9,5},{13,1},{2,14},{6,10},... | collective-permute-start | bytes 98312 | tf_op jit(solution)/shard_map/ppermute | solution.py:472
  20.5 5.0 %collective-permute-start.5 = (bf16[144,256]{1,0:T(8,128)(2,1)S(1)}, bf16[144,256]{1,0:T(8,128)(2,1)S(1)}, u32[]{:S(2)}, u32[]{:S(2)}) collective-permute-start(bf16[144,256]{1,0:T(8,128)(2,1)S(1)} %shard_map.77.tags_ref), channel_id=1, source_target_pairs={{0,16},{16,0},{1,17},{17,1},{2,18},{18,2},{3,19},{19,3},{4,20},{20... | collective-permute-start | bytes 221192 | tf_op jit(solution)/shard_map/ppermute | solution.py:475

commit v6 on v5

--- a/solution.py
+++ b/solution.py
@@ -16,7 +16,7 @@
 
 def row_product_kernel(
     pad_ref, deltas_ref, acts_ref, row_factor_ref, col_factor_ref, queries_ref,
-    out_ref, col_out_ref, early_ref,
+    out_ref, sent_ref, col_out_ref, early_ref,
     pad_in, deltas_in, acts_in, factor_in, sems,
 ):
     steps, tokens, _ = deltas_in.shape
@@ -55,6 +55,7 @@
         return carry
 
     lax.fori_loop(0, steps, step, 0)
+    sent_ref[...] = out_ref[...].astype(BF16)
     col_copy.wait()
     early_copy.wait()
 
@@ -73,11 +74,12 @@
         row_product_kernel,
         out_shape=(
             jax.ShapeDtypeStruct((rows, width), F32),
+            jax.ShapeDtypeStruct((rows, width), BF16),
             jax.ShapeDtypeStruct(col_factor.shape, BF16),
             pltpu.VMEM((early,) + queries.shape[1:], BF16),
         ),
         in_specs=[pl.BlockSpec(memory_space=pl.ANY)] + [hbm] * 5,
-        out_specs=(vmem, vmem, vmem),
+        out_specs=(vmem, vmem, vmem, vmem),
         scratch_shapes=[
             pltpu.SMEM(padding.shape, jnp.int32),
             pltpu.VMEM((steps, tokens // steps, width), BF16),
@@ -97,7 +99,7 @@
     rep, sub, place = (lax.axis_index(a) for a in ("rep", "sub", "wide"))
     half = factor_ref.shape[1]
     rows = mine_ref.shape[0] // wide
-    summed = mine_ref[...] + other_ref[...]
+    summed = mine_ref[...] + other_ref[...].astype(F32)
     high = summed.astype(BF16)
     low = (summed - high.astype(F32)).astype(BF16)
 
@@ -459,13 +461,13 @@
     later = 3 * early
     own_block = lax.dynamic_slice_in_dim(act_factor, lax.axis_index("rep") * half, half, axis=0)
     far_block = lax.ppermute(own_block, "rep", [(0, 1), (1, 0)])
-    mine, columns, first = row_product(
+    mine, rounded, columns, first = row_product(
         padding, deltas[0], activations[0], delta_factor, act_factor, queries, early
     )
-    second = fetch(queries, early, early // 2)
-    third, tags = tagged_fetch(wide, assignment, queries, 3 * early // 2, early // 2)
-    mine, columns, far_block = lax.optimization_barrier((mine, columns, far_block))
-    other = lax.ppermute(mine, "sub", [(0, 1), (1, 0)])
+    second = fetch(queries, early, 32)
+    third, tags = tagged_fetch(wide, assignment, queries, early + 32, 128)
+    rounded, columns, far_block = lax.optimization_barrier((rounded, columns, far_block))
+    other = lax.ppermute(rounded, "sub", [(0, 1), (1, 0)])
     other, second = lax.optimization_barrier((other, second))
     sent = grad_blocks(wide, mine, other, columns, far_block)
     grads = [sent[0]] + [

time: 40.6 us -> 40.1 us (0.988)
    pallas_call x1, Pallas kernels: 1.75 us -> 1.24 us  [fetch(): pl.pallas_call(functools.partial(fetch_kernel, first), out_shape=pltpu.VM...]
    ppermute x3, waiting for transfers between devices: 3.71 us -> 3.27 us  [shared(): lax.ppermute(sent[k], 'wide', [(i, i ^ k) for i in range(wide)])]
    pallas_call x1, Pallas kernels: 1.76 us -> 2.21 us  [tagged_fetch(): pl.pallas_call(functools.partial(tagged_fetch_kernel, first, wide), out_s...]
where the time goes in v6:
time: 40.1 us; the launch traced here: 39.9 us
  Pallas kernels  16 us (40%)
  starting transfers between devices  9.05 us (23%)
  blocking collectives  9.03 us (23%)
  waiting for transfers between devices  3.55 us (9%)
  local copies, waits for them, and re-layouts  1.49 us (4%)
  between operations  0.75 us (2%)
    all_to_all x1, blocking collectives, shared(): lax.all_to_all(partial, ('parts', 'wide', 'rep', 'sub'), split_axis=0, co...  9.03 us
    pallas_call x1, Pallas kernels, shared_scores(): pl.pallas_call(functools.partial(shared_score_kernel, wide, pieces), out_...  5.26 us
    ppermute x3, starting transfers between devices, shared(): lax.ppermute(sent[k], 'wide', [(i, i ^ k) for i in range(wide)])  4.45 us
    pallas_call x1, Pallas kernels, row_product(): pl.pallas_call(row_product_kernel, out_shape=(jax.ShapeDtypeStruct((rows,...  3.45 us
    pallas_call x1, Pallas kernels, local_scores(): pl.pallas_call(functools.partial(local_score_kernel, wide, len(here)), ou...  3.39 us
    ppermute x3, waiting for transfers between devices, shared(): lax.ppermute(sent[k], 'wide', [(i, i ^ k) for i in range(wide)])  3.27 us
    ppermute x1, starting transfers between devices, shared(): far_block = lax.ppermute(own_block, 'rep', [(0, 1), (1, 0)])  3 us
    pallas_call x1, Pallas kernels, tagged_fetch(): pl.pallas_call(functools.partial(tagged_fetch_kernel, first, wide), out_s...  2.21 us
  transfers between devices with their start and end apart: 6, of which 3 were waited for; matrix products, arithmetic and copies ran while one was open for 0% of the time, Pallas kernels for 26%

profile of v6, /device:TPU:0, one launch (start us, length us, event | category | flops | bytes accessed | tf_op | source)
XLA Modules:
  0.0 39.9 jit_solution(2244529017043683989)
XLA Ops:
  0.0 0.9 %constant_dynamic-slice_fusion = bf16[256,256]{1,0:T(8,128)(2,1)S(1)} fusion(bf16[512,256]{1,0:T(8,128)(2,1)} %col_factor_ref.1, s32[]{:T(128)S(6)} %select_n.3), kind=kLoop, calls=%fused_computation | loop fusion | bytes 262148 | tf_op jit(solution)/shard_map/dynamic_slice | solution.py:462
  0.9 3.0 %collective-permute-start = (bf16[256,256]{1,0:T(8,128)(2,1)S(1)}, bf16[256,256]{1,0:T(8,128)(2,1)S(1)}, u32[]{:S(2)}, u32[]{:S(2)}) collective-permute-start(bf16[256,256]{1,0:T(8,128)(2,1)S(1)} %constant_dynamic-slice_fusion), channel_id=1, source_target_pairs={{0,2},{2,0},{1,3},{3,1},{4,6},{6,4},{5,7},{7,5},{8,10},{10,8},{9,1... | collective-permute-start | bytes 393224 | tf_op jit(solution)/shard_map/ppermute | solution.py:463
  4.6 3.4 %shard_map.74 = (f32[256,512]{1,0:T(8,128)S(1)}, bf16[256,512]{1,0:T(8,128)(2,1)S(1)}, bf16[512,256]{1,0:T(8,128)(2,1)S(1)}, bf16[160,64,256]{2,1,0:T(8,128)(2,1)S(1)}) custom-call(s32[1]{0:T(128)S(6)} %copy.8.pad_ref, bf16[1024,512]{1,0:T(8,128)(2,1)} %bitcast.2, bf16[1024,512]{1,0:T(8,128)(2,1)} %bitcast.3, bf16[512,256]{1,0:T(8,128)(2,1)} %row_factor_ref.1, ...), custom_call_target="tpu_custom_call" | custom-call | flops 536870912 | bytes 2097152 | tf_op jit(solution)/shard_map/pallas_call | solution.py:73
  8.0 0.0 collective-permute-done.far_ref
  8.0 0.0 copy-start
  8.0 0.1 collective-permute-start.1
  8.1 1.2 %shard_map.75.refs_5_ = bf16[32,64,256]{2,1,0:T(8,128)(2,1)S(1)} custom-call(bf16[1280,64,256]{2,1,0:T(8,128)(2,1)} %refs_7_.3), custom_call_target="tpu_custom_call" | custom-call | bytes 1048576 | tf_op jit(solution)/shard_map/pallas_call | solution.py:156
  9.4 0.3 collective-permute-done.1.other_ref
  9.6 0.5 %shard_map.76 = (bf16[64,256]{1,0:T(8,128)(2,1)S(1)}, bf16[64,256]{1,0:T(8,128)(2,1)S(1)}, bf16[64,256]{1,0:T(8,128)(2,1)S(1)}, bf16[64,256]{1,0:T(8,128)(2,1)S(1)}) custom-call(f32[256,512]{1,0:T(8,128)S(1)} %get-tuple-element.23.mine_ref, bf16[256,512]{1,0:T(8,128)(2,1)S(1)} %collective-permute-done.1.other_ref, ...), custom_call_target="tpu_custom_call" | custom-call | flops 134217728 | bytes 1572864 | tf_op jit(solution)/shard_map/pallas_call | solution.py:136
  10.1 1.6 %collective-permute-start.2 = (bf16[64,256]{1,0:T(8,128)(2,1)S(1)}, bf16[64,256]{1,0:T(8,128)(2,1)S(1)}, u32[]{:S(2)}, u32[]{:S(2)}) collective-permute-start(bf16[64,256]{1,0:T(8,128)(2,1)S(1)} %get-tuple-element.31), channel_id=1, source_target_pairs={{0,4},{4,0},{8,12},{12,8},{1,5},{5,1},{9,13},{13,9},{2,6},{6,2},{1... | collective-permute-start | bytes 98312 | tf_op jit(solution)/shard_map/ppermute | solution.py:474
  11.8 2.6 %collective-permute-start.3 = (bf16[64,256]{1,0:T(8,128)(2,1)S(1)}, bf16[64,256]{1,0:T(8,128)(2,1)S(1)}, u32[]{:S(2)}, u32[]{:S(2)}) collective-permute-start(bf16[64,256]{1,0:T(8,128)(2,1)S(1)} %get-tuple-element.32), channel_id=1, source_target_pairs={{0,8},{4,12},{8,0},{12,4},{1,9},{5,13},{9,1},{13,5},{2,10},{6,14},... | collective-permute-start | bytes 98312 | tf_op jit(solution)/shard_map/ppermute | solution.py:474
  14.4 0.2 collective-permute-start.4
  14.6 0.0 copy-done
  14.6 2.2 %shard_map.73 = (bf16[128,64,256]{2,1,0:T(8,128)(2,1)S(1)}, bf16[16,256]{1,0:T(8,128)(2,1)S(1)}) custom-call(s32[4]{0:T(128)S(1)} %copy-done, bf16[1280,64,256]{2,1,0:T(8,128)(2,1)} %refs_7_.3), custom_call_target="tpu_custom_call" | custom-call | bytes 4194304 | tf_op jit(solution)/shard_map/pallas_call | solution.py:192
  16.8 0.0 collective-permute-done.2.refs_1_
  16.8 0.3 collective-permute-done.3.refs_2_
  17.1 2.9 %collective-permute-done.4.refs_3_ = bf16[64,256]{1,0:T(8,128)(2,1)S(1)} collective-permute-done((bf16[64,256]{1,0:T(8,128)(2,1)S(1)}, bf16[64,256]{1,0:T(8,128)(2,1)S(1)}, u32[]{:S(2)}, u32[]{:S(2)}) %collective-permute-start.4) | collective-permute-done | bytes 32800 | tf_op jit(solution)/shard_map/ppermute | solution.py:474
  20.1 1.5 %collective-permute-start.5 = (bf16[144,256]{1,0:T(8,128)(2,1)S(1)}, bf16[144,256]{1,0:T(8,128)(2,1)S(1)}, u32[]{:S(2)}, u32[]{:S(2)}) collective-permute-start(bf16[144,256]{1,0:T(8,128)(2,1)S(1)} %shard_map.77.tags_ref), channel_id=1, source_target_pairs={{0,16},{16,0},{1,17},{17,1},{2,18},{18,2},{3,19},{19,3},{4,20},{20... | collective-permute-start | bytes 221192 | tf_op jit(solution)/shard_map/ppermute | solution.py:477
  21.6 3.4 %shard_map.78 = (f32[16,320]{1,0:T(8,128)S(1)}, bf16[480,32,256]{2,1,0:T(8,128)(2,1)S(1)}) custom-call(bf16[144,256]{1,0:T(8,128)(2,1)S(1)} %shard_map.77.tags_ref, bf16[64,256]{1,0:T(8,128)(2,1)S(1)} %get-tuple-element.30.refs_0_, bf16[64,256]{1,0:T(8,128)(2,1)S(1)} %collective-permute-done.2.refs_1_, bf16[64,256]{1,0:T(8,128)(2,1)S(1)} %collective-permute-done.3.refs_2_, ...), custom_call_target="tpu_custom_call" | custom-call | flops 1342177280 | bytes 26214400 | tf_op jit(solution)/shard_map/pallas_call | solution.py:328
  25.0 0.0 collective-permute-done.5.refs_4_
  25.0 5.3 %shard_map.79 = f32[32,1,320]{2,1,0:T(1,128)S(1)} custom-call(bf16[144,256]{1,0:T(8,128)(2,1)S(1)} %shard_map.77.tags_ref, bf16[64,256]{1,0:T(8,128)(2,1)S(1)} %get-tuple-element.30.refs_0_, bf16[64,256]{1,0:T(8,128)(2,1)S(1)} %collective-permute-done.2.refs_1_, bf16[64,256]{1,0:T(8,128)(2,1)S(1)} %collective-permute-done.3.refs_2_, ...), custom_call_target="tpu_custom_call" | custom-call | flops 5368709120 | bytes 15728640 | tf_op jit(solution)/shard_map/pallas_call | solution.py:430
  30.3 9.0 %all_to_all.5 = f32[32,1,320]{2,1,0:T(1,128)S(1)} all-to-all(f32[32,1,320]{2,1,0:T(1,128)S(1)} %shard_map.79), channel_id=1, replica_groups=mesh['parts'=2,'wide'=4,'rep'=2,'sub'=2] {'parts','wide','rep','sub'}, dimensions={0} | all-to-all | bytes 81920 | tf_op jit(solution)/shard_map/all_to_all | solution.py:484
  39.3 0.1 reduce_sum.11
  39.4 0.6 %reduce_sum.12 = f32[1,320]{1,0:T(1,128)} reshape(f32[320]{0:T(512)S(1)} %reduce_sum.11) | data formatting | bytes 2560 | tf_op jit(solution)/shard_map/reduce_sum | solution.py:487
  (1 shorter events, 0.0 us)
Async XLA Ops:
  0.9 7.1 %collective-permute-start = (bf16[256,256]{1,0:T(8,128)(2,1)S(1)}, bf16[256,256]{1,0:T(8,128)(2,1)S(1)}, u32[]{:S(2)}, u32[]{:S(2)}) collective-permute-start(bf16[256,256]{1,0:T(8,128)(2,1)S(1)} %constant_dynamic-slice_fusion), channel_id=1, source_target_pairs={{0,2},{2,0},{1,3},{3,1},{4,6},{6,4},{5,7},{7,5},{8,10},{10,8},{9,1... | collective-permute-start | bytes 393224 | tf_op jit(solution)/shard_map/ppermute | solution.py:463
  8.0 6.5 %copy-start = (s32[4]{0:T(128)S(1)}, s32[4]{0:T(128)}, u32[]{:S(2)}) copy-start(s32[4]{0:T(128)} %order_ref.1) | copy-start | bytes 52
  8.0 1.6 %collective-permute-start.1 = (bf16[256,512]{1,0:T(8,128)(2,1)S(1)}, bf16[256,512]{1,0:T(8,128)(2,1)S(1)}, u32[]{:S(2)}, u32[]{:S(2)}) collective-permute-start(bf16[256,512]{1,0:T(8,128)(2,1)S(1)} %get-tuple-element.26), channel_id=1, source_target_pairs={{0,1},{1,0},{2,3},{3,2},{4,5},{5,4},{6,7},{7,6},{8,9},{9,8},{10,11... | collective-permute-start | bytes 786440 | tf_op jit(solution)/shard_map/ppermute | solution.py:470
  10.1 6.7 %collective-permute-start.2 = (bf16[64,256]{1,0:T(8,128)(2,1)S(1)}, bf16[64,256]{1,0:T(8,128)(2,1)S(1)}, u32[]{:S(2)}, u32[]{:S(2)}) collective-permute-start(bf16[64,256]{1,0:T(8,128)(2,1)S(1)} %get-tuple-element.31), channel_id=1, source_target_pairs={{0,4},{4,0},{8,12},{12,8},{1,5},{5,1},{9,13},{13,9},{2,6},{6,2},{1... | collective-permute-start | bytes 98312 | tf_op jit(solution)/shard_map/ppermute | solution.py:474
  11.8 5.4 %collective-permute-start.3 = (bf16[64,256]{1,0:T(8,128)(2,1)S(1)}, bf16[64,256]{1,0:T(8,128)(2,1)S(1)}, u32[]{:S(2)}, u32[]{:S(2)}) collective-permute-start(bf16[64,256]{1,0:T(8,128)(2,1)S(1)} %get-tuple-element.32), channel_id=1, source_target_pairs={{0,8},{4,12},{8,0},{12,4},{1,9},{5,13},{9,1},{13,5},{2,10},{6,14},... | collective-permute-start | bytes 98312 | tf_op jit(solution)/shard_map/ppermute | solution.py:474
  14.4 5.7 %collective-permute-start.4 = (bf16[64,256]{1,0:T(8,128)(2,1)S(1)}, bf16[64,256]{1,0:T(8,128)(2,1)S(1)}, u32[]{:S(2)}, u32[]{:S(2)}) collective-permute-start(bf16[64,256]{1,0:T(8,128)(2,1)S(1)} %get-tuple-element.33), channel_id=1, source_target_pairs={{0,12},{4,8},{8,4},{12,0},{1,13},{5,9},{9,5},{13,1},{2,14},{6,10},... | collective-permute-start | bytes 98312 | tf_op jit(solution)/shard_map/ppermute | solution.py:474
  20.1 4.9 %collective-permute-start.5 = (bf16[144,256]{1,0:T(8,128)(2,1)S(1)}, bf16[144,256]{1,0:T(8,128)(2,1)S(1)}, u32[]{:S(2)}, u32[]{:S(2)}) collective-permute-start(bf16[144,256]{1,0:T(8,128)(2,1)S(1)} %shard_map.77.tags_ref), channel_id=1, source_target_pairs={{0,16},{16,0},{1,17},{17,1},{2,18},{18,2},{3,19},{19,3},{4,20},{20... | collective-permute-start | bytes 221192 | tf_op jit(solution)/shard_map/ppermute | solution.py:477
